TPU v7x, 256 devices: a whole 4x4x8 slice. The times are simulated.
256 devices in a mesh: ctx: 16 (over y_lo, z), ep: 16 (over y_hi, x, core).
Axes of the slice: x: 4, y: 4 (y_hi: 2, y_lo: 2; y = y_hi * 2 + y_lo), z: 8, core: 2. Of those that a mesh axis runs over, the one named last changes fastest.
Arguments:
- hidden: bfloat16 [2048, 7168], P(('ctx', 'ep')), may hold values from -6 to 6
- q_nope: bfloat16 [2048, 8192], P('ctx', 'ep'), may hold values from -6 to 6
- q_rope: bfloat16 [2048, 4096], P('ctx', 'ep'), may hold values from -100 to 100
- kv_latent: bfloat16 [2048, 512], P('ctx'), may hold values from -6 to 6
- k_rope: bfloat16 [2048, 64], P('ctx'), may hold values from -8 to 8
- key_up: bfloat16 [512, 8192], P(None, 'ep'), may hold values from -0.5 to 0.5
- value_up: bfloat16 [512, 8192], P(None, 'ep'), may hold values from -0.25 to 0.25
- out_proj: bfloat16 [8192, 7168], P(('ep', 'ctx')), may hold values from -0.0625 to 0.0625
- ffn_gain: float32 [7168], replicated, may hold values from 0.5 to 1.5
- router: bfloat16 [7168, 16], replicated, may hold values from -0.0625 to 0.0625
- w_gate: bfloat16 [16, 7168, 2048], P('ep', None, 'ctx'), may hold values from -0.0625 to 0.0625
- w_up: bfloat16 [16, 7168, 2048], P('ep', None, 'ctx'), may hold values from -0.0625 to 0.0625
- w_down: bfloat16 [16, 2048, 7168], P('ep', 'ctx'), may hold values from -0.125 to 0.125
- routes: int32 [2048, 2], P(('ctx', 'ep')), may hold values from 0 to 15, as said below
- load_ema: float32 [16], replicated, may hold values from 0.5 to 1.5
Outputs:
- layer_out: bfloat16 [2048, 7168], P(('ctx', 'ep'))
- new_load: float32 [16], replicated
Inputs may be any that keep to these rules, and one draw needn't show every extreme that they name: In the rows of one device every expert that is named is named by exactly 2 routes; a token's routes name different experts.
All inputs are finite; a program needn't handle non-finite values.
Results may differ from a plain program's by a relative error of at most 0.025.
Values may be sent and summed in bfloat16 or wider, within the bound.
A program may use at most 64 MiB of HBM per device.

v0:
```python
import jax
import jax.numpy as jnp
from jax import lax
from jax.sharding import PartitionSpec as P

D = 7168
KVL = 512
NOPE = 128
ROPE = 64
VDIM = 128
HEAD_DEV = 4


SCORE_FLOOR = -1e30
NORM_EPS = 1e-06
ROUTE_SCALE = 2.5
LOAD_DECAY = 0.5


def absorb_queries(q_nope, key_up):
    row_count = q_nope.shape[0]
    queries = q_nope.reshape(row_count, HEAD_DEV, NOPE)
    key_heads = key_up.reshape(KVL, HEAD_DEV, NOPE)
    return jnp.einsum(
        "thn,khn->thk", queries, key_heads, preferred_element_type=jnp.float32
    ).astype(jnp.bfloat16)


def attend_all(q_latent, q_rotary, positions, kv_latent, k_rope):
    row_count = q_latent.shape[0]
    score_scale = (NOPE + ROPE) ** (-0.5)
    last_query = jnp.max(positions)
    initial = (
        jnp.full((HEAD_DEV, row_count), SCORE_FLOOR, jnp.float32),
        jnp.zeros((HEAD_DEV, row_count), jnp.float32),
        jnp.zeros((HEAD_DEV, row_count, KVL), jnp.float32),
    )
    kv_piece = lax.all_gather(kv_latent, "ctx", axis=0, tiled=True)
    rope_piece = lax.all_gather(k_rope, "ctx", axis=0, tiled=True)

    def compute(current):
        top_old, sum_old, accum_old = current
        key_count = kv_piece.shape[0]
        key_pos = lax.iota(jnp.int32, key_count)
        scores = jnp.einsum("thk,sk->hts", q_latent, kv_piece, preferred_element_type=jnp.float32)
        scores = scores + jnp.einsum(
            "thr,sr->hts", q_rotary, rope_piece, preferred_element_type=jnp.float32
        )
        scores = scores * score_scale
        allowed = key_pos[None, None, :] <= positions[None, :, None]
        scores = jnp.where(allowed, scores, SCORE_FLOOR)
        top_new = jnp.maximum(top_old, jnp.max(scores, axis=2))
        exp_scores = jnp.where(allowed, jnp.exp(scores - top_new[:, :, None]), 0.0)
        sum_new = jnp.sum(exp_scores, axis=2)
        weights = exp_scores.astype(jnp.bfloat16)
        accum_new = jnp.einsum("hts,sk->htk", weights, kv_piece, preferred_element_type=jnp.float32)
        return (top_new, sum_new, accum_new)

    top_scores, sum_exp, accumulated = lax.cond(
        jnp.int32(0) <= last_query, compute, lambda current: current, initial
    )
    return (accumulated / sum_exp[:, :, None]).astype(jnp.bfloat16)


def body(
    hidden,
    q_nope,
    q_rope,
    kv_latent,
    k_rope,
    key_up,
    value_up,
    out_proj,
    ffn_gain,
    router,
    w_gate,
    w_up,
    w_down,
    routes,
    load_ema,
):
    block_rows = q_nope.shape[0]
    ctx_count = lax.axis_size("ctx")
    ctx_index = lax.axis_index("ctx")
    q_latent = absorb_queries(q_nope, key_up)
    q_rotary = q_rope.reshape(block_rows, HEAD_DEV, ROPE)
    own_positions = ctx_index * block_rows + lax.iota(jnp.int32, block_rows)
    latent_out = attend_all(q_latent, q_rotary, own_positions, kv_latent, k_rope)
    value_heads = value_up.reshape(KVL, HEAD_DEV, VDIM)
    head_out = (
        jnp.einsum("htk,kho->tho", latent_out, value_heads, preferred_element_type=jnp.float32)
        .astype(jnp.bfloat16)
        .reshape(block_rows, HEAD_DEV * VDIM)
    )
    projected = jnp.dot(
        head_out,
        lax.all_gather(out_proj, "ctx", axis=0, tiled=True),
        preferred_element_type=jnp.float32,
    )
    attn_sum = lax.psum_scatter(
        projected.astype(jnp.bfloat16), "ep", scatter_dimension=0, tiled=True
    ).astype(jnp.float32)
    residual = (hidden.astype(jnp.float32) + attn_sum).astype(jnp.bfloat16)
    residual_wide = residual.astype(jnp.float32)
    mean_square = jnp.mean(residual_wide * residual_wide, axis=1, keepdims=True)
    normed = (residual_wide * lax.rsqrt(mean_square + NORM_EPS) * ffn_gain).astype(jnp.bfloat16)
    affinity = jax.nn.sigmoid(jnp.dot(normed, router, preferred_element_type=jnp.float32))
    chosen = jnp.take_along_axis(affinity, routes, axis=1)
    gate_weights = ROUTE_SCALE * chosen / jnp.sum(chosen, axis=1, keepdims=True)
    token_count = hidden.shape[0]
    top_count = routes.shape[1]
    expert_count = lax.axis_size("ep")
    capacity = max(2, 2 * token_count * top_count // expert_count)
    pair_expert = routes.reshape(-1)
    expert_ids = lax.iota(jnp.int32, expert_count)
    pair_hits = (pair_expert[:, None] == expert_ids[None, :]).astype(jnp.int32)
    earlier = jnp.cumsum(pair_hits, axis=0) - pair_hits
    pair_rank = jnp.sum(earlier * pair_hits, axis=1)
    pair_slot = pair_expert * capacity + pair_rank
    slot_ids = lax.iota(jnp.int32, expert_count * capacity)
    placing = (
        (slot_ids[:, None] == pair_slot[None, :])
        .astype(jnp.bfloat16)
        .reshape(expert_count * capacity, token_count, top_count)
        .sum(axis=2)
    )
    outgoing = (
        jnp.dot(placing, normed, preferred_element_type=jnp.float32)
        .astype(jnp.bfloat16)
        .reshape(expert_count, capacity, D)
    )
    local_load = jnp.sum(pair_hits, axis=0).astype(jnp.float32)
    total_load = lax.psum(local_load, ("ctx", "ep"))
    arrived = lax.all_to_all(outgoing, "ep", split_axis=0, concat_axis=0, tiled=True).reshape(
        expert_count * capacity, D
    )
    gate_proj = w_gate[0]
    up_proj = w_up[0]
    down_proj = w_down[0]
    slot_rows = lax.all_gather(arrived, "ctx", axis=0, tiled=True)
    gate_part = jnp.dot(slot_rows, gate_proj, preferred_element_type=jnp.float32)
    up_part = jnp.dot(slot_rows, up_proj, preferred_element_type=jnp.float32)
    activations = (jax.nn.silu(gate_part) * up_part).astype(jnp.bfloat16)
    summed = lax.psum_scatter(
        jnp.dot(activations, down_proj, preferred_element_type=jnp.float32).astype(jnp.bfloat16),
        "ctx",
        scatter_dimension=0,
        tiled=True,
    )
    returned = lax.all_to_all(
        summed.reshape(expert_count, capacity, D), "ep", split_axis=0, concat_axis=0, tiled=True
    )
    flat_out = returned.reshape(expert_count * capacity, D)
    picked = (
        jnp.take(flat_out, pair_slot, axis=0).astype(jnp.float32).reshape(token_count, top_count, D)
    )
    routed_sum = jnp.sum(gate_weights[:, :, None] * picked, axis=1)
    layer_out = (residual_wide + routed_sum).astype(jnp.bfloat16)
    mean_load = float(ctx_count * token_count * top_count)
    new_load = LOAD_DECAY * load_ema + (1.0 - LOAD_DECAY) * total_load / mean_load
    return (layer_out, new_load)


def solution(mesh):
    placed = (
        P(("ctx", "ep"), None),
        P("ctx", "ep"),
        P("ctx", "ep"),
        P("ctx", None),
        P("ctx", None),
        P(None, "ep"),
        P(None, "ep"),
        P(("ep", "ctx"), None),
        P(),
        P(),
        P("ep", None, "ctx"),
        P("ep", None, "ctx"),
        P("ep", "ctx", None),
        P(("ctx", "ep"), None),
        P(),
    )
    return jax.shard_map(
        body, mesh=mesh, in_specs=placed, out_specs=(P(("ctx", "ep"), None), P()), check_vma=False
    )
```

profile of v0, /device:TPU:1, one launch (start us, length us, event | category | flops | bytes accessed | tf_op | source)
XLA Modules:
  0.0 545.8 jit_solution(6954617254886872292)
XLA Ops:
  7.2 0.0 copy-start
  7.2 0.0 all-gather.4.cloned.1.call-start
  7.2 0.7 all-gather.4.cloned.1.call-update
  7.9 0.0 all-gather.6.cloned.1.call-start
  8.0 0.7 all-gather.6.cloned.1.call-update
  8.7 0.0 reduce-scatter.3.cloned.1.call-start
  8.7 0.6 fusion.52
  10.0 1.3 copy.60
  11.3 33.0 %all_gather.13 = bf16[2048,64]{0,1:T(8,128)(2,1)S(1)} all-gather(bf16[128,64]{0,1:T(8,128)(2,1)} %param.21), channel_id=1, replica_groups=mesh['ctx'=16,'ep'=16] {'ctx'}, dimensions={0}, use_global_device_ids=true | all-gather | bytes 278528 | tf_op jit(solution)/shard_map/all_gather | solution.py:39
  44.3 1.4 fusion.17
  45.6 31.5 %all-gather.4.cloned.1.call-done = bf16[2048,512]{1,0:T(8,128)(2,1)} async-done(((bf16[128,512]{1,0:T(8,128)(2,1)}), bf16[2048,512]{1,0:T(8,128)(2,1)}) %all-gather.4.cloned.1.call-update) | async-done | bytes 2097168 | tf_op jit(solution)/shard_map/all_gather | solution.py:38
  77.1 11.6 %conditional.1 = (f32[4,128]{1,0:T(4,128)S(1)}, f32[4,128,512]{2,1,0:T(8,128)}) conditional(s32[]{:T(128)} %convert_element_type.68, () %tuple.16, (s32[128]{0:T(128)S(1)}, bf16[2048,512]{1,0:T(8,128)(2,1)}, bf16[128,4,512]{0,2,1:T(8,128)(2,1)S(1)}, bf16[128,256]{1,0:T(8,128)(2,1)}, bf16[2048,64]{0,1:T(8,128)(2,1)S(1)}) %tuple.17), branch_computations={%region_1.0_spmd, %region_2.5_spmd} | conditional | flops 2292448768 | bytes 36909640 | solution.py:59
  77.1 0.2 iota_compare_fusion
  77.3 4.9 fusion.5
  82.3 0.0 copy-done.5
  82.3 0.1 copy.48
  82.4 0.0 copy-start.1
  82.4 3.2 fusion.55
  85.6 2.3 fusion.2
  87.9 0.8 fusion.1
  88.7 1.6 convolution_convert_fusion.4
  90.3 85.1 %all-gather.6.cloned.1.call-done = bf16[512,7168]{1,0:T(8,128)(2,1)} async-done(((bf16[32,7168]{1,0:T(8,128)(2,1)}), bf16[512,7168]{1,0:T(8,128)(2,1)}) %all-gather.6.cloned.1.call-update) | async-done | bytes 7340048 | tf_op jit(solution)/shard_map/all_gather | solution.py:97
  175.4 5.6 %convolution_convert_fusion.1 = bf16[128,7168]{1,0:T(8,128)(2,1)} fusion(bf16[128,512]{0,1:T(8,128)(2,1)S(1)} %bitcast.68, bf16[512,7168]{1,0:T(8,128)(2,1)} %all-gather.6.cloned.1.call-done), kind=kOutput, calls=%fused_computation.18 | convolution fusion | flops 940441600 | bytes 9306112 | tf_op jit(solution)/shard_map/dot_general | solution.py:95
  181.0 0.0 reduce-scatter.3.cloned.1.call-update
  181.0 0.0 all-gather.8.cloned.1.call-start
  181.1 0.0 copy-done.6
  181.1 0.1 copy.50
  181.2 0.1 reshape.156
  181.3 0.1 fusion.45
  181.4 0.2 fusion.47
  181.5 0.1 reduce_sum.73
  181.6 0.1 copy.57
  181.7 0.1 fusion.48
  181.8 72.6 %reduce-scatter.3.cloned.1.call-done = bf16[8,7168]{1,0:T(8,128)(2,1)} async-done(((bf16[128,7168]{1,0:T(8,128)(2,1)}), bf16[8,7168]{1,0:T(8,128)(2,1)}) %reduce-scatter.3.cloned.1.call-update) | async-done | bytes 114704 | tf_op jit(solution)/shard_map/reduce_scatter | solution.py:100
  254.5 1.1 fusion.36
  255.5 0.3 convolution_convert_fusion.2
  255.9 0.2 reshape.157
  256.1 17.4 %all_to_all.10 = bf16[16,2,7168]{2,1,0:T(2,128)(2,1)S(1)} all-to-all(bf16[16,2,7168]{2,1,0:T(2,128)(2,1)S(1)} %reshape.157), channel_id=1, replica_groups=mesh['ctx'=16,'ep'=16] {'ep'}, dimensions={0} | all-to-all | bytes 917504 | tf_op jit(solution)/shard_map/all_to_all | solution.py:134
  273.4 0.9 reshape.158
  274.3 0.0 all-gather.8.cloned.1.call-update
  274.4 0.2 reduce-scatter.5.cloned.1.call-start
  274.6 87.9 %all-gather.8.cloned.1.call-done = bf16[512,7168]{1,0:T(8,128)(2,1)} async-done(((bf16[32,7168]{1,0:T(8,128)(2,1)}), bf16[512,7168]{1,0:T(8,128)(2,1)}) %all-gather.8.cloned.1.call-update) | async-done | bytes 7340048 | tf_op jit(solution)/shard_map/all_gather | solution.py:140
  362.5 5.6 %fusion.15 = f32[512,128]{1,0:T(8,128)S(1)} fusion(bf16[512,7168]{1,0:T(8,128)(2,1)} %all-gather.8.cloned.1.call-done, bf16[1,7168,128]{2,1,0:T(8,128)(2,1)} %param.27), kind=kOutput, calls=%fused_computation.23 | convolution fusion | flops 939524096 | bytes 9437184 | tf_op jit(solution)/shard_map/dot_general | solution.py:141
  368.2 15.3 %convolution_convert_fusion = bf16[512,7168]{1,0:T(8,128)(2,1)} fusion(bf16[1,128,7168]{2,1,0:T(8,128)(2,1)S(1)} %copy-done, bf16[512,7168]{1,0:T(8,128)(2,1)} %all-gather.8.cloned.1.call-done, bf16[1,7168,128]{2,1,0:T(8,128)(2,1)} %param.28, f32[512,128]{1,0:T(8,128)S(1)} %fusion.15), kind=kOutput, calls=%fused_computation.17 | convolution fusion | flops 1883111424 | bytes 18612224 | tf_op jit(solution)/shard_map/dot_general | solution.py:145
  383.5 0.0 reduce-scatter.5.cloned.1.call-update
  383.6 135.0 %psum.7 = f32[16]{0:T(128)S(1)} all-reduce(f32[16]{0:T(128)S(1)} %convert_element_type.86), channel_id=1, replica_groups=mesh['ctx'=16,'ep'=16] {'ctx','ep'}, use_global_device_ids=true, to_apply=%region_14.15 | all-reduce | flops 16 | bytes 128 | tf_op jit(solution)/shard_map/psum | solution.py:133
  518.6 0.1 mul.87
  518.7 0.1 copy.53
  518.8 0.1 copy.54
  518.9 0.1 reshape.169
  519.0 0.5 multiply_add_fusion
  519.5 2.0 reshape.159
  521.5 5.0 all-to-all-start.1
  526.5 0.3 fusion.28
  526.7 0.7 gather_fusion.1
  527.4 0.1 reshape.172
  527.5 0.1 fusion.50
  527.6 0.1 multiply_divide_fusion
  527.7 9.2 %all-to-all-done.1 = bf16[16,2,7168]{2,1,0:T(2,128)(2,1)S(1)} async-done(((bf16[16,2,7168]{2,1,0:T(2,128)(2,1)}), bf16[16,2,7168]{2,1,0:T(2,128)(2,1)S(1)}, u32[]{:S(2)}, u32[]{:S(2)}) %all-to-all-start.1) | async-done | bytes 458784 | tf_op jit(solution)/shard_map/all_to_all | solution.py:150
  536.9 0.2 reshape.160
  537.1 0.7 gather_fusion
  537.8 0.1 gather.12
  537.9 0.7 multiply_reduce_fusion
  538.6 0.7 fusion.39
  (23 shorter events, 0.1 us)
Async XLA Ops:
  7.2 361.0 %copy-start = (bf16[1,128,7168]{2,1,0:T(8,128)(2,1)S(1)}, bf16[1,128,7168]{2,1,0:T(8,128)(2,1)}, u32[]{:S(2)}) copy-start(bf16[1,128,7168]{2,1,0:T(8,128)(2,1)} %param.29) | copy-start | bytes 5505028
  7.2 70.0 %all-gather.4.cloned.1.call-start = ((), (), s32[]{:S(2)}) async-start(), calls=%async_computation.4 | async-start | bytes 2228224 | tf_op jit(solution)/shard_map/all_gather | solution.py:38
  7.9 167.5 %all-gather.6.cloned.1.call-start = ((), (), s32[]{:S(2)}) async-start(), calls=%async_computation.5 | async-start | bytes 7798784 | tf_op jit(solution)/shard_map/all_gather | solution.py:97
  8.7 245.8 %reduce-scatter.3.cloned.1.call-start = ((), (), s32[]{:S(2)}) async-start(), calls=%async_computation.6 | async-start | bytes 1949696 | tf_op jit(solution)/shard_map/reduce_scatter | solution.py:100
  77.1 5.1 copy-start.5
  82.4 3.3 copy-start.1
  175.4 5.7 %copy-start.6 = (s32[8,2]{0,1:T(2,128)S(1)}, s32[8,2]{0,1:T(2,128)}, u32[]{:S(2)}) copy-start(s32[8,2]{0,1:T(2,128)} %param.30) | copy-start | bytes 196
  175.4 79.1 %copy-start.4 = (bf16[8,7168]{1,0:T(8,128)(2,1)S(1)}, bf16[8,7168]{1,0:T(8,128)(2,1)}, u32[]{:S(2)}) copy-start(bf16[8,7168]{1,0:T(8,128)(2,1)} %param.17) | copy-start | bytes 344068
  175.4 80.1 %copy-start.3 = (f32[7168]{0:T(1024)S(1)}, f32[7168]{0:T(1024)}, u32[]{:S(2)}) copy-start(f32[7168]{0:T(1024)} %param.25) | copy-start | bytes 86020
  181.0 181.5 %all-gather.8.cloned.1.call-start = ((), (), s32[]{:S(2)}) async-start(), calls=%async_computation.7 | async-start | bytes 7798784 | tf_op jit(solution)/shard_map/all_gather | solution.py:140
  274.4 245.1 %reduce-scatter.5.cloned.1.call-start = ((), (), s32[]{:S(2)}) async-start(), calls=%async_computation.8 | async-start | bytes 7798784 | tf_op jit(solution)/shard_map/reduce_scatter | solution.py:144
  383.5 135.4 %copy-start.7 = (f32[16]{0:T(128)S(1)}, f32[16]{0:T(128)}, u32[]{:S(2)}) copy-start(f32[16]{0:T(128)} %param.31) | copy-start | bytes 196
  383.5 143.0 %copy-start.2 = (bf16[7168,16]{0,1:T(8,128)(2,1)S(1)}, bf16[7168,16]{0,1:T(8,128)(2,1)}, u32[]{:S(2)}) copy-start(bf16[7168,16]{0,1:T(8,128)(2,1)} %param.26) | copy-start | bytes 688132
  521.5 15.5 %all-to-all-start.1 = ((bf16[16,2,7168]{2,1,0:T(2,128)(2,1)}), bf16[16,2,7168]{2,1,0:T(2,128)(2,1)S(1)}, u32[]{:S(2)}, u32[]{:S(2)}) async-start(bf16[16,2,7168]{2,1,0:T(2,128)(2,1)} %reshape.159), calls=%async_computation.3 | async-start | bytes 917504 | tf_op jit(solution)/shard_map/all_to_all | solution.py:150
Sparse Core Ops, SparseCore 0:
  9.8 67.2 all-gather.3
  78.9 96.4 all-gather.5
  181.1 73.2 reduce-scatter.2
  274.5 87.9 all-gather.7
  383.7 86.0 reduce-scatter.4
where the time goes:
time: 546 us
  waiting for transfers between devices  288 us (53%)
  blocking collectives  185 us (34%)
  matrix products  40.6 us (7%)
  between operations  14.6 us (3%)
  local copies, waits for them, and re-layouts  6.82 us (1%)
    psum x1, blocking collectives, body(): total_load = lax.psum(local_load, ('ctx', 'ep'))  135 us
    all_gather x1, waiting for transfers between devices, body(): slot_rows = lax.all_gather(arrived, 'ctx', axis=0, tiled=True)  87.9 us
    all_gather x1, waiting for transfers between devices, body(): lax.all_gather(out_proj, 'ctx', axis=0, tiled=True)  85.1 us
    reduce_scatter x1, waiting for transfers between devices, body(): lax.psum_scatter(projected.astype(jnp.bfloat16), 'ep', scatter_dimension=...  72.6 us
    all_gather x1, blocking collectives, attend_all(): rope_piece = lax.all_gather(k_rope, 'ctx', axis=0, tiled=True)  33 us
    all_gather x1, waiting for transfers between devices, attend_all(): kv_piece = lax.all_gather(kv_latent, 'ctx', axis=0, tiled=True)  31.5 us
    all_to_all x1, blocking collectives, body(): lax.all_to_all(outgoing, 'ep', split_axis=0, concat_axis=0, tiled=True)  17.4 us
    dot_general x1, matrix products, body(): jnp.dot(activations, down_proj, preferred_element_type=jnp.float32)  15.3 us
  transfers between devices with their start and end apart: 6, of which 5 were waited for; matrix products, arithmetic and copies ran while one was open for 4% of the time, Pallas kernels for 0%

commit v1 on v0

v1 whole, which is shorter than its diff:
```python
import functools

import jax
import jax.numpy as jnp
from jax import lax
from jax.experimental import pallas as pl
from jax.experimental.pallas import tpu as pltpu
from jax.sharding import PartitionSpec as P

D = 7168
KVL = 512
NOPE = 128
ROPE = 64
VDIM = 128
HEAD_DEV = 4
SL = 896
EXPERTS = 16
META = 128

SCORE_FLOOR = -1e30
NORM_EPS = 1e-06
ROUTE_SCALE = 2.5
LOAD_DECAY = 0.5
MESH = pl.DeviceIdType.MESH
BF = jnp.bfloat16
F32 = jnp.float32
VMEM_LIMIT = 56 * 2**20


def place():
    c = lax.axis_index("ctx")
    e = lax.axis_index("ep")
    return c, e, lax.div(c, 8), lax.rem(c, 8), lax.div(e, 2), lax.rem(e, 2)


def remote(src, dst, send, recv, device):
    return pltpu.make_async_remote_copy(
        src_ref=src, dst_ref=dst, send_sem=send, recv_sem=recv, device_id=device, device_id_type=MESH
    )


def dot(a, b):
    return jnp.dot(a, b, preferred_element_type=F32)


def dot_t(a, b):
    return lax.dot_general(a, b, (((1,), (1,)), ((), ())), preferred_element_type=F32)


def iota(shape, dim):
    return lax.broadcasted_iota(jnp.int32, shape, dim)


def selector(rows, columns, shift, width):
    row, column = iota((rows, columns), 0), iota((rows, columns), 1)
    return jnp.where((row == column + shift) & (column < width), 1.0, 0.0).astype(BF)


def column_of(block, index):
    return jnp.sum(jnp.where(iota(block.shape, 1) == index, block, 0.0), axis=1, keepdims=True)


def attention_kernel(
    q_nope, q_rope, kv, k_rope, key_up, value_up, out_proj, hidden, routes, w_gate, w_up,
    attn_out, hidden_out, wgu,
    KV, Q, top, total, accum, HO, WO, PB, SB, RED, RK, TS, TR, HS, HR,
    kv_s, kv_r, kf_s, kf_r, op_s, op_r, hd_s, hd_r, w_s, w_r, wf_s, wf_r,
    hp_s, hm_s, ho_r, sb_s, sb_r, rk_s, rk_r, t_s, t_r, local,
):
    c, e, yl, z, k, s = place()
    sib = 2 * k + 1 - s
    e_half, e_row = lax.div(e, 8), lax.rem(e, 8)
    turned = (yl * 8 + k, 2 * z + s)

    KV[pl.ds(pl.multiple_of(c * 128, 128), 128), 0:KVL] = kv[...]
    KV[pl.ds(pl.multiple_of(c * 128, 128), 128), KVL:640] = dot(
        k_rope[...], selector(ROPE, 128, 0, ROPE)
    ).astype(BF)

    @pl.when(lax.rem(c, 2) == 0)
    def _():
        KV[pl.ds(pl.multiple_of((c + 1) * 128, 128), 128), :] = jnp.zeros((128, 640), BF)

    route_block = jnp.where(
        iota((8, META), 1) == 0,
        routes[:, 0:1],
        jnp.where(iota((8, META), 1) == 1, routes[:, 1:2], 0),
    ).astype(F32)
    for kk in range(8):
        HS[kk, :, 0:SL] = hidden[:, kk * SL : (kk + 1) * SL].astype(F32)
        HS[kk, :, SL:1024] = route_block

    barrier = pltpu.get_barrier_semaphore()
    for d in range(1, 16):
        pl.semaphore_signal(barrier, 1, device_id=(lax.rem(c + d, 16), e), device_id_type=MESH)
        pl.semaphore_signal(barrier, 1, device_id=(c, lax.rem(e + d, 16)), device_id_type=MESH)

    @pl.when(z != k)
    def _():
        pl.semaphore_signal(barrier, 1, device_id=turned, device_id_type=MESH)

    pl.semaphore_wait(barrier, 30 + (z != k).astype(jnp.int32))

    def kv_copy(d):
        half = KV.at[pl.ds(pl.multiple_of(c * 128 + s * 64, 64), 64), :]
        return remote(half, half, kv_s.at[d], kv_r.at[c], (c + d, e))

    for d in range(1, 16):

        @pl.when(c + d < 16)
        def _():
            kv_copy(d).start()

    def hidden_copy(kk):
        return remote(
            HS.at[kk], HR.at[e_row], hd_s.at[kk], hd_r.at[e_row], (c, 2 * kk + e_half)
        )

    for kk in range(8):

        @pl.when(2 * kk + e_half != e)
        def _():
            hidden_copy(kk).start()

        @pl.when(2 * kk + e_half == e)
        def _():
            HR[e_row] = HS[kk]

    def proj_copy(d):
        cc = lax.rem(c + d, 16)
        zz = lax.rem(cc, 8)
        return remote(
            out_proj.at[:, pl.ds(pl.multiple_of(zz * SL, 128), SL)],
            WO.at[pl.ds(pl.multiple_of(c * 32, 32), 32), :],
            op_s.at[d],
            op_r.at[c],
            (cc, e),
        )

    own_proj = pltpu.make_async_copy(
        out_proj.at[:, pl.ds(pl.multiple_of(z * SL, 128), SL)],
        WO.at[pl.ds(pl.multiple_of(c * 32, 32), 32), :],
        local.at[0],
    )
    own_proj.start()
    for d in range(1, 16):
        proj_copy(d).start()

    def weight_copy(d, which):
        kk = lax.rem(k + d, 8)
        source = (w_gate, w_up)[which]
        return remote(
            source.at[0, pl.ds(pl.multiple_of(kk * SL, SL), SL), :],
            wgu.at[e, :, pl.ds(which * 128, 128)],
            w_s.at[d, which],
            w_r.at[k, which],
            (c, 2 * kk + s),
        )

    def own_weight(which):
        source = (w_gate, w_up)[which]
        return pltpu.make_async_copy(
            source.at[0, pl.ds(pl.multiple_of(k * SL, SL), SL), :],
            wgu.at[e, :, pl.ds(which * 128, 128)],
            local.at[1 + which],
        )

    for which in range(2):
        own_weight(which).start()
    for d in range(1, 8):
        for which in range(2):
            weight_copy(d, which).start()

    for h in range(HEAD_DEV):
        rows, columns = slice(h * 128, (h + 1) * 128), slice(h * 128, (h + 1) * 128)
        Q[rows, 0:KVL] = dot_t(q_nope[:, columns], key_up[:, columns]).astype(BF)
        Q[rows, KVL:640] = dot(
            q_rope[...], selector(HEAD_DEV * ROPE, 128, h * ROPE, ROPE)
        ).astype(BF)
    top[...] = jnp.full(top.shape, SCORE_FLOOR, F32)
    total[...] = jnp.zeros(total.shape, F32)
    accum[...] = jnp.zeros(accum.shape, F32)

    def half_block(j, core):
        return KV.at[pl.ds(pl.multiple_of(j * 128 + core * 64, 64), 64), :]

    def kv_forward(j, core):
        half = half_block(j, core)
        return remote(half, half, kf_s.at[j], kf_r.at[j], (c, sib))

    def pass_on(p):
        for j in (2 * p + 1, 2 * p):

            @pl.when((p >= 0) & (j < c))
            def _():
                half = half_block(j, s)
                remote(half, half, kv_s.at[0], kv_r.at[j], (c, e)).wait_recv()
                kv_forward(j, s).start()

    score_scale = (NOPE + ROPE) ** (-0.5)

    def attend(p):
        for j in (2 * p + 1, 2 * p):

            @pl.when(j < c)
            def _():
                kv_forward(j, 1 - s).wait_recv()

        keys = KV[pl.ds(pl.multiple_of(p * 256, 256), 256), :]
        scores = dot_t(Q[...], keys)
        query_pos = c * 128 + (iota(scores.shape, 0) & 127)
        key_pos = p * 256 + iota(scores.shape, 1)
        scores = jnp.where(key_pos <= query_pos, scores, SCORE_FLOOR)
        top_old = top[...]
        top_new = jnp.maximum(top_old, jnp.max(scores, axis=1, keepdims=True))
        exp_scores = jnp.exp((scores - top_new) * score_scale)
        shrink = jnp.exp((top_old - top_new) * score_scale)
        top[...] = top_new
        total[...] = total[...] * shrink + jnp.sum(exp_scores, axis=1, keepdims=True)
        accum[...] = accum[...] * shrink + dot(exp_scores.astype(BF), keys[:, 0:KVL])

    last = lax.div(c, 2)
    pass_on(last)
    pass_on(last - 1)

    def attention_step(i, carry):
        attend(last - i)
        pass_on(last - i - 2)
        return carry

    lax.fori_loop(0, last + 1, attention_step, 0)

    own_rows = pl.ds(pl.multiple_of(z * 128, 128), 128)
    for h in range(HEAD_DEV):
        rows, columns = slice(h * 128, (h + 1) * 128), slice(h * 128, (h + 1) * 128)
        latent = (accum[rows, :] / total[rows, :]).astype(BF)
        HO[own_rows, columns] = dot(latent, value_up[:, columns]).astype(BF)

    def ho_copy(zz, half, up):
        block = HO.at[pl.ds(pl.multiple_of(zz * 128 + half * 64, 64), 64), :]
        target = yl * 8 + lax.rem(z + (1 if up else 7), 8)
        return remote(
            block, block, (hp_s if up else hm_s).at[zz, half], ho_r.at[zz, half], (target, e)
        )

    for half in range(2):
        ho_copy(z, half, True).start()
        ho_copy(z, half, False).start()
    own_proj.wait()
    for d in range(1, 16):
        cc = lax.rem(c + d, 16)
        remote(
            out_proj.at[:, pl.ds(0, SL)],
            WO.at[pl.ds(pl.multiple_of(cc * 32, 32), 32), :],
            op_s.at[0],
            op_r.at[cc],
            (c, e),
        ).wait_recv()

    def sib_copy(zz, core):
        return remote(
            PB.at[zz, pl.ds(pl.multiple_of((1 - core) * 64, 64), 64), :],
            SB.at[zz],
            sb_s.at[zz],
            sb_r.at[zz],
            (c, sib),
        )

    def project(zz):
        PB[zz] = dot(HO[pl.ds(pl.multiple_of(zz * 128, 128), 128), :], WO[...]).astype(BF)
        sib_copy(zz, s).start()

    def chip_copy(zz):
        return remote(RED.at[zz], RK.at[k], rk_s.at[zz], rk_r.at[k], (c, 2 * zz + s))

    def reduce_pair(zz):
        sib_copy(zz, s).wait_recv()
        own = PB[zz, pl.ds(pl.multiple_of(s * 64, 64), 64), :]
        RED[zz] = (own.astype(F32) + SB[zz].astype(F32)).astype(BF)

        @pl.when(zz != k)
        def _():
            chip_copy(zz).start()

        @pl.when(zz == k)
        def _():
            RK[k] = RED[zz]

    project(z)
    waiting = z
    for t in range(1, 5):
        below, above = lax.rem(z + 8 - t, 8), lax.rem(z + t, 8)
        for half in range(2):
            ho_copy(below, half, True).wait_recv()
            if t < 4:
                ho_copy(below, half, True).start()
        project(below)
        reduce_pair(waiting)
        waiting = below
        if t < 4:
            for half in range(2):
                ho_copy(above, half, False).wait_recv()
                if t < 3:
                    ho_copy(above, half, False).start()
            project(above)
            reduce_pair(waiting)
            waiting = above
    reduce_pair(waiting)

    for d in range(1, 8):
        kk = lax.rem(k + d, 8)
        remote(RED.at[0], RK.at[kk], rk_s.at[0], rk_r.at[kk], (c, e)).wait_recv()
    summed = RK[0].astype(F32)
    for kk in range(1, 8):
        summed = summed + RK[kk].astype(F32)
    TS[...] = summed.astype(BF)

    def turn_copy():
        return remote(TS, TR, t_s.at[0], t_r.at[0], turned)

    @pl.when(z != k)
    def _():
        turn_copy().start()

    for which in range(2):
        own_weight(which).wait()

    def forward_copy(kk, core):
        expert = 2 * kk + core
        return remote(wgu.at[expert], wgu.at[expert], wf_s.at[kk], wf_r.at[kk], (c, sib))

    forward_copy(k, s).start()
    for d in range(1, 8):
        kk = lax.rem(k + d, 8)
        for which in range(2):
            piece = wgu.at[2 * kk + s, :, pl.ds(which * 128, 128)]
            remote(piece, piece, w_s.at[0, which], w_r.at[kk, which], (c, e)).wait_recv()
        forward_copy(kk, s).start()

    for j in range(8):

        @pl.when(8 * s + j != e)
        def _():
            remote(HS.at[0], HR.at[j], hd_s.at[0], hd_r.at[j], (c, e)).wait_recv()

    hidden_out[...] = HR[...].reshape(64, 1024)

    @pl.when(z != k)
    def _():
        turn_copy().wait_recv()
        attn_out[...] = TR[...]

    @pl.when(z == k)
    def _():
        attn_out[...] = TS[...]

    for kk in range(8):
        forward_copy(kk, 1 - s).wait_recv()

    for d in range(1, 16):

        @pl.when(c + d < 16)
        def _():
            kv_copy(d).wait_send()

        proj_copy(d).wait_send()

    for j in range(15):

        @pl.when(j < c)
        def _():
            kv_forward(j, s).wait_send()

    for kk in range(8):

        @pl.when(2 * kk + e_half != e)
        def _():
            hidden_copy(kk).wait_send()

        forward_copy(kk, s).wait_send()
        sib_copy(kk, s).wait_send()

        @pl.when(kk != k)
        def _():
            chip_copy(kk).wait_send()

    for d in range(1, 8):
        for which in range(2):
            weight_copy(d, which).wait_send()
    for half in range(2):
        for t in range(0, 4):
            ho_copy(lax.rem(z + 8 - t, 8), half, True).wait_send()
        for t in range(0, 3):
            ho_copy(lax.rem(z + t, 8), half, False).wait_send()

    @pl.when(z != k)
    def _():
        turn_copy().wait_send()


def experts_kernel(
    attn, hidden, router, gain, wgu, w_down,
    act_out, meta_out, residual_out, wd,
    X, W, RT, GN, ST, XC, acc0, acc1, HS, HR, A,
    local, st_s, st_r, w_s, w_r, wf_s, wf_r, xp_s, xm_s, xy_s, x_r, h_s, h_r, a_s, a_r,
):
    c, e, yl, z, k, s = place()
    sib = 2 * k + 1 - s
    c_y = (1 - yl) * 8 + z
    c_up = yl * 8 + lax.rem(z + 1, 8)
    c_down = yl * 8 + lax.rem(z + 7, 8)

    fetch_router = pltpu.make_async_copy(
        router.at[pl.ds(pl.multiple_of(k * SL, SL), SL), :], RT, local.at[0]
    )
    fetch_gain = pltpu.make_async_copy(gain.at[k], GN, local.at[1])
    fetch_wgu = pltpu.make_async_copy(wgu, W, local.at[2])
    own_down = pltpu.make_async_copy(
        w_down.at[0, :, pl.ds(pl.multiple_of(k * SL, 128), SL)],
        wd.at[pl.ds(pl.multiple_of(e * 128, 128), 128), :],
        local.at[3],
    )
    fetch_router.start()
    fetch_gain.start()
    own_down.start()

    barrier = pltpu.get_barrier_semaphore()
    for d in range(1, 8):
        pl.semaphore_signal(
            barrier, 1, device_id=(c, 2 * lax.rem(k + d, 8) + s), device_id_type=MESH
        )
    pl.semaphore_signal(barrier, 1, device_id=(c, sib), device_id_type=MESH)
    for neighbour in (c_y, c_up, c_down):
        pl.semaphore_signal(barrier, 1, device_id=(neighbour, e), device_id_type=MESH)
    fetch_router.wait()
    fetch_gain.wait()
    fetch_wgu.start()

    residual = (hidden[:, 0:SL] + attn[...].astype(F32)).astype(BF).astype(F32)
    residual_out[...] = residual
    gains = GN[...]
    lane = iota((64, META), 1)
    padded_router = dot(RT[...], selector(EXPERTS, META, 0, EXPERTS)).astype(BF)
    logits = dot((residual * gains).astype(BF), padded_router)
    squares = jnp.sum(residual * residual, axis=1, keepdims=True)
    ST[k] = jnp.where(lane == EXPERTS, squares, logits)
    pl.semaphore_wait(barrier, 11)

    def stat_copy(d):
        kk = lax.rem(k + d, 8)
        return remote(ST.at[k], ST.at[k], st_s.at[d], st_r.at[k], (c, 2 * kk + s))

    for d in range(1, 8):
        stat_copy(d).start()

    def down_copy(d):
        kk = lax.rem(k + d, 8)
        return remote(
            w_down.at[0, :, pl.ds(pl.multiple_of(kk * SL, 128), SL)],
            wd.at[pl.ds(pl.multiple_of(e * 128, 128), 128), :],
            w_s.at[d],
            w_r.at[k],
            (c, 2 * kk + s),
        )

    for d in range(1, 8):
        down_copy(d).start()
    for d in range(1, 8):
        kk = lax.rem(k + d, 8)
        remote(ST.at[kk], ST.at[kk], st_s.at[0], st_r.at[kk], (c, e)).wait_recv()
    stats = ST[0]
    for kk in range(1, 8):
        stats = stats + ST[kk]
    inverse = lax.rsqrt(column_of(stats, EXPERTS) / D + NORM_EPS)
    normed = (residual * inverse * gains).astype(BF)
    affinity = 1.0 / (1.0 + jnp.exp(-(stats * inverse)))
    routed = hidden[:, SL:1024]
    route0, route1 = column_of(routed, 0), column_of(routed, 1)
    lane_f = lane.astype(F32)
    chosen0 = jnp.sum(jnp.where(lane_f == route0, affinity, 0.0), axis=1, keepdims=True)
    chosen1 = jnp.sum(jnp.where(lane_f == route1, affinity, 0.0), axis=1, keepdims=True)
    scale = ROUTE_SCALE / (chosen0 + chosen1)
    meta = jnp.where(lane == 0, route0, jnp.where(lane == 1, route1, 0.0))
    for index, weight in ((2, chosen0 * scale), (4, chosen1 * scale)):
        coarse = weight.astype(BF).astype(F32)
        meta = jnp.where(lane == index, coarse, meta)
        meta = jnp.where(lane == index + 1, weight - coarse, meta)

    def rows_of(cc):
        return pl.ds(pl.multiple_of(cc * 64, 64), 64)

    X[rows_of(c), 0:SL] = normed
    X[rows_of(c), SL:1024] = meta.astype(BF)

    def row_copy(cc, way):
        block = X.at[rows_of(cc), :]
        target = {"y": c_y, "up": c_up, "down": c_down}[way]
        sems = {"y": xy_s, "up": xp_s, "down": xm_s}[way]
        return remote(block, block, sems.at[cc], x_r.at[cc], (target, e))

    row_copy(c, "y").start()
    row_copy(c, "up").start()
    row_copy(c, "down").start()
    row_copy(c_y, "y").wait_recv()
    row_copy(c_y, "up").start()
    row_copy(c_y, "down").start()

    def block_of(y, zz):
        return y * 8 + zz

    def arrive(zz, way, go_on):
        for y in (yl, 1 - yl):
            row_copy(block_of(y, zz), way).wait_recv()
            if go_on:
                row_copy(block_of(y, zz), way).start()

    def half_copy(zz):
        return remote(HS.at[zz], HR.at[k], h_s.at[zz], h_r.at[k], (c, 2 * zz + s))

    def first_layers(za, zb):
        places = [(0, za), (1, za), (0, zb), (1, zb)]
        for i, (y, zz) in enumerate(places):
            XC[i * 64 : (i + 1) * 64, :] = X[rows_of(block_of(y, zz)), :]
        acc0[...] = jnp.zeros(acc0.shape, F32)
        acc1[...] = jnp.zeros(acc1.shape, F32)
        routed_here = XC[:, SL:1024].astype(F32)
        r0, r1 = column_of(routed_here, 0), column_of(routed_here, 1)

        def one_expert(expert, carry):
            part = dot(XC[:, 0:SL], W[expert])
            number = expert.astype(F32)
            acc0[...] += jnp.where(r0 == number, part, 0.0)
            acc1[...] += jnp.where(r1 == number, part, 0.0)
            return carry

        lax.fori_loop(0, EXPERTS, one_expert, 0)
        for i, (y, zz) in enumerate(places):
            HS[zz, y, 0] = acc0[i * 64 : (i + 1) * 64, :].astype(BF)
            HS[zz, y, 1] = acc1[i * 64 : (i + 1) * 64, :].astype(BF)
        for zz in (za, zb):

            @pl.when(zz != k)
            def _():
                half_copy(zz).start()

            @pl.when(zz == k)
            def _():
                HR[k] = HS[zz]

    near = [lax.rem(z + 8 - t, 8) for t in range(5)]
    far = [lax.rem(z + t, 8) for t in range(4)]
    arrive(near[1], "up", True)
    arrive(far[1], "down", True)
    fetch_wgu.wait()
    first_layers(z, near[1])
    arrive(near[2], "up", True)
    arrive(far[2], "down", True)
    first_layers(far[1], near[2])
    arrive(near[3], "up", True)
    arrive(far[3], "down", False)
    first_layers(far[2], near[3])
    arrive(near[4], "up", False)
    first_layers(far[3], near[4])
    meta_out[...] = X[:, SL:1024]

    for d in range(1, 8):
        kk = lax.rem(k + d, 8)
        remote(HS.at[0], HR.at[kk], h_s.at[0], h_r.at[kk], (c, e)).wait_recv()
    for y in range(2):
        meta_here = X[rows_of(block_of(y, k)), SL:1024].astype(F32)
        for r in range(2):
            both = HR[0, y, r].astype(F32)
            for kk in range(1, 8):
                both = both + HR[kk, y, r].astype(F32)
            weight = column_of(meta_here, 2 + 2 * r) + column_of(meta_here, 3 + 2 * r)
            gate, up = both[:, 0:128], both[:, 128:256]
            A[k, y, r] = (gate / (1.0 + jnp.exp(-gate)) * up * weight).astype(BF)

    def act_copy(d):
        kk = lax.rem(k + d, 8)
        return remote(A.at[k], A.at[k], a_s.at[d], a_r.at[k], (c, 2 * kk + s))

    for d in range(1, 8):
        act_copy(d).start()

    own_down.wait()

    def forward_copy(kk, core):
        block = wd.at[pl.ds(pl.multiple_of((2 * kk + core) * 128, 128), 128), :]
        return remote(block, block, wf_s.at[kk], wf_r.at[kk], (c, sib))

    forward_copy(k, s).start()
    for d in range(1, 8):
        kk = lax.rem(k + d, 8)
        block = wd.at[pl.ds(pl.multiple_of((2 * kk + s) * 128, 128), 128), :]
        remote(block, block, w_s.at[0], w_r.at[kk], (c, e)).wait_recv()
        forward_copy(kk, s).start()
    for d in range(1, 8):
        kk = lax.rem(k + d, 8)
        remote(A.at[kk], A.at[kk], a_s.at[0], a_r.at[kk], (c, e)).wait_recv()
    act_out[...] = A[...]
    for kk in range(8):
        forward_copy(kk, 1 - s).wait_recv()

    for d in range(1, 8):
        stat_copy(d).wait_send()
        down_copy(d).wait_send()
        act_copy(d).wait_send()
    for kk in range(8):
        forward_copy(kk, s).wait_send()

        @pl.when(kk != k)
        def _():
            half_copy(kk).wait_send()

    row_copy(c, "y").wait_send()
    for y in (yl, 1 - yl):
        for t in range(4):
            row_copy(block_of(y, near[t]), "up").wait_send()
        for t in range(3):
            row_copy(block_of(y, far[t]), "down").wait_send()


def down_kernel(
    act, meta, residual, wd, ema,
    layer_out, load_out,
    WD, AC, DP, RP, RM, SP, SM, YS, YR, OS, OR, CS, CR,
    local, p_s, p_r, m_s, m_r, y_s, y_r, o_s, o_r, c_s, c_r,
):
    c, e, yl, z, k, s = place()
    sib = 2 * k + 1 - s
    c_y = (1 - yl) * 8 + z
    c_up = yl * 8 + lax.rem(z + 1, 8)
    c_down = yl * 8 + lax.rem(z + 7, 8)
    e_half = lax.div(e, 8)

    fetch = pltpu.make_async_copy(wd, WD, local.at[0])
    fetch.start()
    barrier = pltpu.get_barrier_semaphore()
    pl.semaphore_signal(barrier, 1, device_id=(c, sib), device_id_type=MESH)
    for neighbour in (c_y, c_up, c_down):
        pl.semaphore_signal(barrier, 1, device_id=(neighbour, e), device_id_type=MESH)
    for kk in range(8):

        @pl.when(2 * kk + e_half != e)
        def _():
            pl.semaphore_signal(barrier, 1, device_id=(c, 2 * kk + e_half), device_id_type=MESH)

    pl.semaphore_wait(barrier, 12 - (e_half == s).astype(jnp.int32))

    routed = meta[...].astype(F32)
    lane_f = iota(routed.shape, 1).astype(F32)
    named = jnp.where(lane_f == column_of(routed, 0), 1.0, 0.0) + jnp.where(
        lane_f == column_of(routed, 1), 1.0, 0.0
    )
    CS[...] = jnp.broadcast_to(jnp.sum(named, axis=0, keepdims=True), CS.shape)
    count_copy = remote(CS, CR, c_s.at[0], c_r.at[0], (c, sib))
    count_copy.start()
    fetch.wait()

    def second_layer(za, zb):
        places = [(0, za), (1, za), (0, zb), (1, zb)]
        for i, (y, zz) in enumerate(places):
            rows = slice(i * 64, (i + 1) * 64)
            here = meta[pl.ds(pl.multiple_of((y * 8 + zz) * 64, 64), 64), :].astype(F32)
            r0, r1 = column_of(here, 0), column_of(here, 1)
            a0, a1 = act[zz, y, 0].astype(F32), act[zz, y, 1].astype(F32)
            for expert in range(EXPERTS):
                picked = jnp.where(r0 == float(expert), a0, 0.0) + jnp.where(
                    r1 == float(expert), a1, 0.0
                )
                AC[rows, expert * 128 : (expert + 1) * 128] = picked.astype(BF)
        out = dot(AC[...], WD[...])
        for i, (y, zz) in enumerate(places):
            DP[zz, y] = out[i * 64 : (i + 1) * 64, :].astype(BF)

    def up_copy(source, step, y):
        return remote(source, RP.at[step, y], p_s.at[step, y], p_r.at[step, y], (c_up, e))

    def down_copy(source, step, y):
        return remote(source, RM.at[step, y], m_s.at[step, y], m_r.at[step, y], (c_down, e))

    ups = [lax.rem(z + 4 - t, 8) for t in range(5)]
    downs = [lax.rem(z + 5 + t, 8) for t in range(4)]
    second_layer(ups[0], downs[0])
    for y in range(2):
        up_copy(DP.at[ups[0], y], 0, y).start()
        down_copy(DP.at[downs[0], y], 0, y).start()
    for t in range(1, 4):
        second_layer(ups[t], downs[t])
        for y in range(2):
            up_copy(SP.at[0, y], t - 1, y).wait_recv()
            SP[t - 1, y] = (DP[ups[t], y].astype(F32) + RP[t - 1, y].astype(F32)).astype(BF)
            up_copy(SP.at[t - 1, y], t, y).start()
            if t < 3:
                down_copy(SM.at[0, y], t - 1, y).wait_recv()
                SM[t - 1, y] = (DP[downs[t], y].astype(F32) + RM[t - 1, y].astype(F32)).astype(BF)
                down_copy(SM.at[t - 1, y], t, y).start()

    def final(y):
        return DP[z, y].astype(F32) + RP[3, y].astype(F32) + RM[2, y].astype(F32)

    for y in (1 - yl, yl):
        down_copy(SM.at[0, 0], 2, y).wait_recv()
        up_copy(SP.at[0, 0], 3, y).wait_recv()
        if y is yl:
            break
        YS[...] = final(y).astype(BF)
        y_copy = remote(YS, YR, y_s.at[0], y_r.at[0], (c_y, e))
        y_copy.start()
    own = final(yl) + residual[...]
    y_copy.wait_recv()
    OS[...] = own + YR[...].astype(F32)

    def owner_copy(j):
        return remote(
            OS.at[pl.ds(j * 8, 8), :], OR.at[k], o_s.at[j], o_r.at[k], (c, 8 * s + j)
        )

    for j in range(8):

        @pl.when(8 * s + j != e)
        def _():
            owner_copy(j).start()

        @pl.when(8 * s + j == e)
        def _():
            OR[k] = OS[pl.ds(j * 8, 8), :]

    count_copy.wait_recv()
    counts = (CS[...] + CR[...])[0:1, 0:EXPERTS]
    load_out[...] = LOAD_DECAY * ema[...] + (1.0 - LOAD_DECAY) * counts / 256.0

    for kk in range(8):

        @pl.when(2 * kk + e_half != e)
        def _():
            remote(
                OS.at[pl.ds(0, 8), :], OR.at[kk], o_s.at[0], o_r.at[kk], (c, e)
            ).wait_recv()

        layer_out[:, kk * SL : (kk + 1) * SL] = OR[kk].astype(BF)

    for y in range(2):
        up_copy(DP.at[ups[0], y], 0, y).wait_send()
        down_copy(DP.at[downs[0], y], 0, y).wait_send()
        for t in range(1, 4):
            up_copy(SP.at[t - 1, y], t, y).wait_send()
            if t < 3:
                down_copy(SM.at[t - 1, y], t, y).wait_send()
    y_copy.wait_send()
    count_copy.wait_send()
    for j in range(8):

        @pl.when(8 * s + j != e)
        def _():
            owner_copy(j).wait_send()


def in_vmem(count):
    return [pl.BlockSpec(memory_space=pltpu.VMEM)] * count


def anywhere(count):
    return [pl.BlockSpec(memory_space=pl.ANY)] * count


def dma(*shape):
    return pltpu.SemaphoreType.DMA(shape)


def shaped(shape, dtype):
    return jax.ShapeDtypeStruct(shape, dtype)


def params(number):
    return pltpu.CompilerParams(
        collective_id=number, has_side_effects=True, vmem_limit_bytes=VMEM_LIMIT
    )


def body(
    hidden, q_nope, q_rope, kv_latent, k_rope, key_up, value_up, out_proj, ffn_gain, router,
    w_gate, w_up, w_down, routes, load_ema,
):
    v = pltpu.VMEM
    attn, rows, wgu = pl.pallas_call(
        attention_kernel,
        out_shape=(shaped((64, SL), BF), shaped((64, 1024), F32), shaped((16, SL, 256), BF)),
        in_specs=in_vmem(6) + anywhere(1) + in_vmem(2) + anywhere(2),
        out_specs=tuple(in_vmem(2) + anywhere(1)),
        scratch_shapes=[
            v((2048, 640), BF), v((512, 640), BF), v((512, 1), F32), v((512, 1), F32),
            v((512, 512), F32), v((1024, 512), BF), v((512, SL), BF), v((8, 128, SL), BF),
            v((8, 64, SL), BF), v((8, 64, SL), BF), v((8, 64, SL), BF), v((64, SL), BF),
            v((64, SL), BF), v((8, 8, 1024), F32), v((8, 8, 1024), F32),
            dma(16), dma(16), dma(16), dma(16), dma(16), dma(16), dma(8), dma(8),
            dma(8, 2), dma(8, 2), dma(8), dma(8), dma(8, 2), dma(8, 2), dma(8, 2),
            dma(8), dma(8), dma(8), dma(8), dma(1), dma(1), dma(3),
        ],
        compiler_params=params(0),
        name="attention",
    )(q_nope, q_rope, kv_latent, k_rope, key_up, value_up, out_proj, hidden, routes, w_gate, w_up)
    act, meta, residual, wd = pl.pallas_call(
        experts_kernel,
        out_shape=(
            shaped((8, 2, 2, 64, 128), BF),
            shaped((1024, META), BF),
            shaped((64, SL), F32),
            shaped((2048, SL), BF),
        ),
        in_specs=in_vmem(2) + anywhere(4),
        out_specs=tuple(in_vmem(3) + anywhere(1)),
        scratch_shapes=[
            v((1024, 1024), BF), v((16, SL, 256), BF), v((SL, EXPERTS), BF), v((1, SL), F32),
            v((8, 64, META), F32), v((256, 1024), BF), v((256, 256), F32), v((256, 256), F32),
            v((8, 2, 2, 64, 256), BF), v((8, 2, 2, 64, 256), BF), v((8, 2, 2, 64, 128), BF),
            dma(4), dma(8), dma(8), dma(8), dma(8), dma(8), dma(8), dma(16), dma(16), dma(16),
            dma(16), dma(8), dma(8), dma(8), dma(8),
        ],
        compiler_params=params(1),
        name="experts",
    )(attn, rows, router, ffn_gain.reshape(8, 1, SL), wgu, w_down)
    layer_out, new_load = pl.pallas_call(
        down_kernel,
        out_shape=(shaped((8, D), BF), shaped((1, EXPERTS), F32)),
        in_specs=in_vmem(3) + anywhere(1) + in_vmem(1),
        out_specs=tuple(in_vmem(2)),
        scratch_shapes=[
            v((2048, SL), BF), v((256, 2048), BF), v((8, 2, 64, SL), BF), v((4, 2, 64, SL), BF),
            v((3, 2, 64, SL), BF), v((3, 2, 64, SL), BF), v((2, 2, 64, SL), BF), v((64, SL), BF),
            v((64, SL), BF), v((64, SL), F32), v((8, 8, SL), F32), v((8, 128), F32),
            v((8, 128), F32),
            dma(1), dma(4, 2), dma(4, 2), dma(3, 2), dma(3, 2), dma(1), dma(1), dma(8), dma(8),
            dma(1), dma(1),
        ],
        compiler_params=params(2),
        name="second_layer",
    )(act, meta, residual, wd, load_ema.reshape(1, EXPERTS))
    return layer_out, new_load.reshape(EXPERTS)


def solution(mesh):
    placed = (
        P(("ctx", "ep"), None),
        P("ctx", "ep"),
        P("ctx", "ep"),
        P("ctx", None),
        P("ctx", None),
        P(None, "ep"),
        P(None, "ep"),
        P(("ep", "ctx"), None),
        P(),
        P(),
        P("ep", None, "ctx"),
        P("ep", None, "ctx"),
        P("ep", "ctx", None),
        P(("ctx", "ep"), None),
        P(),
    )
    return jax.shard_map(
        body, mesh=mesh, in_specs=placed, out_specs=(P(("ctx", "ep"), None), P()), check_vma=False
    )
```

time: 546 us -> 244 us (0.45)
  waiting for transfers between devices: 288 us -> 0 us
  Pallas kernels: 0 us -> 234 us
  blocking collectives: 185 us -> 0 us
  matrix products: 40.6 us -> 0 us
  between operations: 14.6 us -> 0.66 us
    pallas_call x0 -> x3, Pallas kernels: none -> 234 us  [the longest x1 100 us: body(): pl.pallas_call(attention_kernel, out_shape=(shaped((64, SL), BF), shaped(...]
    all_gather x3 -> x0, waiting for transfers between devices: 204 us -> none  [the longest x1 87.9 us: body(): slot_rows = lax.all_gather(arrived, 'ctx', axis=0, tiled=True)]
    psum x1 -> x0, blocking collectives: 135 us -> none  [body(): total_load = lax.psum(local_load, ('ctx', 'ep'))]
    reduce_scatter x2 -> x0, waiting for transfers between devices: 72.6 us -> none  [the longest x1 72.6 us: body(): lax.psum_scatter(projected.astype(jnp.bfloat16), 'ep', scatter_dimension=...]
    dot_general x10 -> x0, matrix products: 40.6 us -> none  [the longest x1 15.3 us: body(): jnp.dot(activations, down_proj, preferred_element_type=jnp.float32)]
    all_gather x1 -> x0, blocking collectives: 33 us -> none  [attend_all(): rope_piece = lax.all_gather(k_rope, 'ctx', axis=0, tiled=True)]
    all_to_all x1 -> x0, blocking collectives: 17.4 us -> none  [body(): lax.all_to_all(outgoing, 'ep', split_axis=0, concat_axis=0, tiled=True)]
    all_to_all x1 -> x0, waiting for transfers between devices: 9.23 us -> none  [body(): lax.all_to_all(summed.reshape(expert_count, capacity, D), 'ep', split_axi...]
  transfers between devices with their start and end apart: 6 -> 0, of which waited for: 5 -> 0; matrix products, arithmetic and copies ran while one was open for 4% -> 0% of each run, Pallas kernels for 0% -> 0%
where the time goes in v1:
time: 244 us; the launch traced here: 243 us
  Pallas kernels  234 us (96%)
  local copies, waits for them, and re-layouts  7.99 us (3%)
    pallas_call x1, Pallas kernels, body(): pl.pallas_call(attention_kernel, out_shape=(shaped((64, SL), BF), shaped(...  100 us
    pallas_call x1, Pallas kernels, body(): pl.pallas_call(experts_kernel, out_shape=(shaped((8, 2, 2, 64, 128), BF),...  90.8 us
    pallas_call x1, Pallas kernels, body(): pl.pallas_call(down_kernel, out_shape=(shaped((8, D), BF), shaped((1, EXP...  43.3 us
    unnamed x5, local copies, waits for them, and re-layouts  7.99 us

profile of v1, /device:TPU:1, one launch (start us, length us, event | category | flops | bytes accessed | tf_op | source)
XLA Modules:
  0.0 243.1 jit_solution(15643513589997755833)
XLA Ops:
  0.6 1.3 copy.18.routes
  2.0 1.4 copy.17.k_rope
  3.4 2.5 %copy.19.router = bf16[7168,16]{1,0:T(8,128)(2,1)} copy(bf16[7168,16]{0,1:T(8,128)(2,1)} %param.24) | data formatting | bytes 458752 | tf_op args[9]
  5.9 100.3 %attention.1 = (bf16[64,896]{1,0:T(8,128)(2,1)}, f32[64,1024]{1,0:T(8,128)}, bf16[16,896,256]{2,1,0:T(8,128)(2,1)}) custom-call(bf16[128,512]{1,0:T(8,128)(2,1)} %q_nope.1, bf16[128,256]{1,0:T(8,128)(2,1)} %q_rope.1, bf16[128,512]{1,0:T(8,128)(2,1)} %kv.1, bf16[128,64]{1,0:T(8,128)(2,1)} %copy.17.k_rope, bf16[512,512]{1,0:T(8,128)(2,1)} %key_up.1, ...), custom_call_target="tpu_custom_call" | custom-call | tf_op jit(solution)/shard_map/attention/pallas_call | solution.py:787
  106.2 90.8 %experts.1 = (bf16[8,2,2,64,128]{4,3,2,1,0:T(8,128)(2,1)}, bf16[1024,128]{1,0:T(8,128)(2,1)}, f32[64,896]{1,0:T(8,128)}, bf16[2048,896]{1,0:T(8,128)(2,1)}) custom-call(bf16[64,896]{1,0:T(8,128)(2,1)} %get-tuple-element.11.attn, f32[64,1024]{1,0:T(8,128)} %get-tuple-element.12.hidden, bf16[7168,16]{1,0:T(8,128)(2,1)} %copy.19.router, f32[8,1,896]{2,1,0:T(1,128)} %bitcast.3, ...), custom_call_target="tpu_custom_call" | custom-call | tf_op jit(solution)/shard_map/experts/pallas_call | solution.py:804
  197.0 43.3 %second_layer.1 = (bf16[8,7168]{1,0:T(8,128)(2,1)}, f32[1,16]{1,0:T(1,128)}) custom-call(bf16[8,2,2,64,128]{4,3,2,1,0:T(8,128)(2,1)} %get-tuple-element.14.act, bf16[1024,128]{1,0:T(8,128)(2,1)} %get-tuple-element.15.meta, f32[64,896]{1,0:T(8,128)} %get-tuple-element.16.residual, bf16[2048,896]{1,0:T(8,128)(2,1)} %get-tuple-element.17.wd, f32[1,16]{1,0:T(1,128)} %bitcast.4), custom_call_target="tpu_custom_call" | custom-call | tf_op jit(solution)/shard_map/second_layer/pallas_call | solution.py:824
  240.3 1.6 copy.22
  241.9 1.2 copy.23

commit v2 on v0

v2 whole, which is shorter than its diff:
```python
import functools

import jax
import jax.numpy as jnp
from jax import lax
from jax.experimental import pallas as pl
from jax.experimental.pallas import tpu as pltpu
from jax.sharding import PartitionSpec as P

D = 7168
KVL = 512
NOPE = 128
ROPE = 64
VDIM = 128
HEAD_DEV = 4
SL = 896
EXPERTS = 16
META = 128
TOKENS = 64

SCORE_FLOOR = -1e30
NORM_EPS = 1e-06
ROUTE_SCALE = 2.5
LOAD_DECAY = 0.5
MESH = pl.DeviceIdType.MESH
BF = jnp.bfloat16
F32 = jnp.float32
VMEM_LIMIT = 56 * 2**20


def place():
    c = lax.axis_index("ctx")
    e = lax.axis_index("ep")
    return c, e, lax.div(c, 8), lax.rem(c, 8), lax.div(e, 2), lax.rem(e, 2)


def remote(src, dst, send, recv, device):
    return pltpu.make_async_remote_copy(
        src_ref=src, dst_ref=dst, send_sem=send, recv_sem=recv, device_id=device, device_id_type=MESH
    )


def dot(a, b):
    return jnp.dot(a, b, preferred_element_type=F32)


def dot_t(a, b):
    return lax.dot_general(a, b, (((1,), (1,)), ((), ())), preferred_element_type=F32)


def iota(shape, dim):
    return lax.broadcasted_iota(jnp.int32, shape, dim)


def selector(rows, columns, shift, width):
    row, column = iota((rows, columns), 0), iota((rows, columns), 1)
    return jnp.where((row == column + shift) & (column < width), 1.0, 0.0).astype(BF)


def column_of(block, index):
    return jnp.sum(jnp.where(iota(block.shape, 1) == index, block, 0.0), axis=1, keepdims=True)


def layer_kernel(
    q_nope, q_rope, kv, k_rope, key_up, value_up, hidden, routes, gain, ema, out_proj, router, w_gate, w_up, w_down,
    layer_out, load_out,
    KV, Q, top, total, accum, HO, WO, PB, SB, RED, RK, TS, TR, HS, HR,
    X, W, RT, ST, XC, acc0, acc1, GS, GR, A, WD, AC, DP, YB, RP, RM, SP, SM, YS, YR, OS, OR, CS, CR,
    local, kp_s, km_s, ky_s, kv_r, kf_s, kf_r, op_s, op_r, oy_s, oy_r, hd_s, hd_r,
    w_s, w_r, wf_s, wf_r, hp_s, hm_s, ho_r, sb_s, sb_r, rk_s, rk_r, t_s, t_r,
    st_s, st_r, d_s, d_r, df_s, df_r, xp_s, xm_s, xy_s, x_r, g_s, g_r, a_s, a_r,
    yb_s, yb_r, p_s, p_r, m_s, m_r, y_s, y_r, o_s, o_r, c_s, c_r,
):
    c, e, yl, z, k, s = place()
    sib = 2 * k + 1 - s
    e_half, e_row = lax.div(e, 8), lax.rem(e, 8)
    c_y = (1 - yl) * 8 + z
    sign = 1 - 2 * s

    def along(t):
        return lax.rem(z + 8 + sign * t, 8)

    c_up, c_down = yl * 8 + along(1), yl * 8 + along(-1)
    near = [along(-t) for t in range(5)]
    far = [along(t) for t in range(4)]

    def kv_rows(slot, start, size):
        return pl.ds(pl.multiple_of(slot * 128 + start, 64), size)

    def kv_slot(y, zz):
        return 2 * zz + y

    own_slot = kv_slot(yl, z)
    KV[kv_rows(own_slot, 0, 128), 0:KVL] = kv[...]
    KV[kv_rows(own_slot, 0, 128), KVL:640] = lax.dot_general(
        k_rope[...], selector(ROPE, 128, 0, ROPE), (((0,), (0,)), ((), ())),
        preferred_element_type=F32,
    ).astype(BF)

    @pl.when(yl == 0)
    def _():
        for zz in range(8):
            KV[kv_rows(kv_slot(1, zz), 0, 128), :] = jnp.zeros((128, 640), BF)

    diagonal = iota((8, 8), 0) == iota((8, 8), 1)
    route_columns = [
        jnp.sum(jnp.where(diagonal, routes[r : r + 1, :], 0), axis=1, keepdims=True)
        for r in range(2)
    ]
    route_block = jnp.where(
        iota((8, META), 1) == 0,
        route_columns[0],
        jnp.where(iota((8, META), 1) == 1, route_columns[1], 0),
    ).astype(F32)
    for kk in range(8):
        HS[kk, :, 0:SL] = hidden[:, kk * SL : (kk + 1) * SL].astype(F32)
        HS[kk, :, SL:1024] = route_block

    barrier = pltpu.get_barrier_semaphore()

    def greet(device):
        pl.semaphore_signal(barrier, 1, device_id=device, device_id_type=MESH)

    for d in range(1, 8):
        greet((yl * 8 + lax.rem(z + d, 8), e))
    greet((c_y, e))
    for d in range(1, 16):
        greet((c, lax.rem(e + d, 16)))
    turn_base = jnp.where(lax.rem(z + 8 - k, 8) < 4, 0, 4)
    turn_self = (z == k) & (k < 4)
    for q in range(4):

        @pl.when(jnp.logical_not((z == k) & (turn_base + q == k)))
        def _():
            greet((yl * 8 + k, 2 * (turn_base + q) + s))

    pl.semaphore_wait(barrier, 27 - turn_self.astype(jnp.int32))

    def kv_copy(y, zz, way):
        block = KV.at[kv_rows(kv_slot(y, zz), s * 64, 64), :]
        target = {"y": c_y, "up": c_up, "down": c_down}[way]
        sems = {"y": ky_s, "up": kp_s, "down": km_s}[way]
        slot = kv_slot(y, zz)
        return remote(block, block, sems.at[slot], kv_r.at[slot], (target, e))

    def kv_share(y, zz, core):
        slot = kv_slot(y, zz)
        block = KV.at[kv_rows(slot, core * 64, 64), :]
        return remote(block, block, kf_s.at[slot], kf_r.at[slot], (c, sib))

    kv_copy(yl, z, "up").start()
    kv_copy(yl, z, "down").start()

    @pl.when(yl == 0)
    def _():
        kv_copy(0, z, "y").start()

    def proj_copy(d):
        zz = lax.rem(z + d, 8)
        return remote(
            out_proj.at[:, pl.ds(pl.multiple_of(zz * SL, 128), SL)],
            WO.at[pl.ds(pl.multiple_of(c * 32, 32), 32), :],
            op_s.at[d],
            op_r.at[z],
            (yl * 8 + zz, e),
        )

    own_proj = pltpu.make_async_copy(
        out_proj.at[:, pl.ds(pl.multiple_of(z * SL, 128), SL)],
        WO.at[pl.ds(pl.multiple_of(c * 32, 32), 32), :],
        local.at[0],
    )
    own_proj.start()
    for d in range(1, 8):
        proj_copy(d).start()

    def hidden_copy(kk):
        return remote(
            HS.at[kk], HR.at[e_row], hd_s.at[kk], hd_r.at[e_row], (c, 2 * kk + e_half)
        )

    for kk in range(8):

        @pl.when(2 * kk + e_half != e)
        def _():
            hidden_copy(kk).start()

        @pl.when(2 * kk + e_half == e)
        def _():
            HR[e_row] = HS[kk]

    def weight_copy(d, which):
        kk = lax.rem(k + d, 8)
        source = (w_gate, w_up)[which]
        return remote(
            source.at[0, pl.ds(pl.multiple_of(kk * SL, SL), SL), :],
            W.at[e, :, pl.ds(which * 128, 128)],
            w_s.at[d, which],
            w_r.at[k, which],
            (c, 2 * kk + s),
        )

    def own_weight(which):
        source = (w_gate, w_up)[which]
        return pltpu.make_async_copy(
            source.at[0, pl.ds(pl.multiple_of(k * SL, SL), SL), :],
            W.at[e, :, pl.ds(which * 128, 128)],
            local.at[1 + which],
        )

    for which in range(2):
        own_weight(which).start()
    for d in range(1, 8):
        for which in range(2):
            weight_copy(d, which).start()
    RT[...] = jnp.zeros(RT.shape, BF)
    fetch_router = pltpu.make_async_copy(
        router.at[:, pl.ds(pl.multiple_of(k * SL, 128), SL)], RT.at[pl.ds(0, EXPERTS), :], local.at[3]
    )
    fetch_router.start()

    def down_rows(expert):
        return pl.ds(pl.multiple_of(expert * 128, 128), 128)

    def down_weight(d):
        kk = lax.rem(k + d, 8)
        return remote(
            w_down.at[0, :, pl.ds(pl.multiple_of(kk * SL, 128), SL)],
            WD.at[down_rows(e), :],
            d_s.at[d],
            d_r.at[k],
            (c, 2 * kk + s),
        )

    own_down = pltpu.make_async_copy(
        w_down.at[0, :, pl.ds(pl.multiple_of(k * SL, 128), SL)], WD.at[down_rows(e), :], local.at[4]
    )
    own_down.start()

    for h in range(HEAD_DEV):
        rows, columns = slice(h * 128, (h + 1) * 128), slice(h * 128, (h + 1) * 128)
        Q[rows, 0:KVL] = dot_t(q_nope[:, columns], key_up[:, columns]).astype(BF)
        Q[rows, KVL:640] = dot(
            q_rope[...], selector(HEAD_DEV * ROPE, 128, h * ROPE, ROPE)
        ).astype(BF)
    top[...] = jnp.full(top.shape, SCORE_FLOOR, F32)
    total[...] = jnp.zeros(total.shape, F32)
    accum[...] = jnp.zeros(accum.shape, F32)

    @pl.when(yl == 1)
    def _():
        kv_copy(0, z, "y").wait_recv()
        kv_share(0, z, s).start()

        @pl.when(s == 1)
        def _():
            kv_copy(0, z, "up").start()
            kv_copy(0, z, "down").start()

    def kv_arrive(zz, way, go_on):
        kv_copy(yl, zz, way).wait_recv()
        if go_on:
            kv_copy(yl, zz, way).start()
        kv_share(yl, zz, s).start()

        @pl.when((yl == 0) & (s == 0))
        def _():
            kv_copy(0, zz, "y").start()

        @pl.when(yl == 1)
        def _():
            kv_copy(0, zz, way).wait_recv()
            kv_share(0, zz, s).start()
            if go_on:

                @pl.when(s == 1)
                def _():
                    kv_copy(0, zz, way).start()

    score_scale = (NOPE + ROPE) ** (-0.5)

    def attend(zz, own):
        if not own:
            kv_share(yl, zz, 1 - s).wait_recv()

        @pl.when(yl == 1)
        def _():
            kv_share(0, zz, 1 - s).wait_recv()

        @pl.when((yl == 1) | (zz <= z))
        def _():
            keys = KV[pl.ds(pl.multiple_of(zz * 256, 256), 256), :]
            scores = dot_t(Q[...], keys)
            query_pos = c * 128 + (iota(scores.shape, 0) & 127)
            column = iota(scores.shape, 1)
            key_pos = zz * 128 + jnp.where(column < 128, column, column + (1024 - 128))
            scores = jnp.where(key_pos <= query_pos, scores, SCORE_FLOOR)
            top_old = top[...]
            top_new = jnp.maximum(top_old, jnp.max(scores, axis=1, keepdims=True))
            exp_scores = jnp.exp((scores - top_new) * score_scale)
            shrink = jnp.exp((top_old - top_new) * score_scale)
            top[...] = top_new
            total[...] = total[...] * shrink + jnp.sum(exp_scores, axis=1, keepdims=True)
            accum[...] = accum[...] * shrink + dot(exp_scores.astype(BF), keys[:, 0:KVL])

    def proj_piece(zz):
        piece = WO.at[pl.ds(pl.multiple_of((yl * 8 + zz) * 32, 32), 32), :]
        return remote(out_proj.at[:, pl.ds(0, SL)], piece, op_s.at[0], op_r.at[zz], (c, e))

    def proj_share(y):
        row = WO.at[pl.ds(pl.multiple_of(y * 256, 256), 256), :]
        return remote(row, row, oy_s.at[0], oy_r.at[0], (c_y, e))

    kv_arrive(near[1], "up", True)
    kv_arrive(far[1], "down", True)
    attend(z, True)
    kv_arrive(near[2], "up", True)
    kv_arrive(far[2], "down", True)
    attend(near[1], False)
    attend(far[1], False)
    kv_arrive(near[3], "up", True)
    kv_arrive(far[3], "down", False)
    attend(near[2], False)
    attend(far[2], False)
    kv_arrive(near[4], "up", False)
    own_proj.wait()
    for d in range(1, 8):
        proj_piece(lax.rem(z + d, 8)).wait_recv()
    proj_share(yl).start()
    attend(near[3], False)
    attend(far[3], False)
    attend(near[4], False)

    own_rows = pl.ds(pl.multiple_of(z * 128, 128), 128)
    for h in range(HEAD_DEV):
        rows, columns = slice(h * 128, (h + 1) * 128), slice(h * 128, (h + 1) * 128)
        latent = (accum[rows, :] / total[rows, :]).astype(BF)
        HO[own_rows, columns] = dot(latent, value_up[:, columns]).astype(BF)

    def ho_copy(zz, half, up):
        block = HO.at[pl.ds(pl.multiple_of(zz * 128 + half * 64, 64), 64), :]
        target = yl * 8 + lax.rem(z + (1 if up else 7), 8)
        return remote(
            block, block, (hp_s if up else hm_s).at[zz, half], ho_r.at[zz, half], (target, e)
        )

    for half in range(2):
        ho_copy(z, half, True).start()
        ho_copy(z, half, False).start()
    proj_share(1 - yl).wait_recv()

    def ho_arrive(zz, up, go_on):
        for half in range(2):
            ho_copy(zz, half, up).wait_recv()
            if go_on:
                ho_copy(zz, half, up).start()

    def sib_copy(zz):
        return remote(
            PB.at[zz, pl.ds(pl.multiple_of((1 - s) * 64, 64), 64), :],
            SB.at[zz],
            sb_s.at[zz],
            sb_r.at[zz],
            (c, sib),
        )

    below = [lax.rem(z + 8 - t, 8) for t in range(5)]
    above = [lax.rem(z + t, 8) for t in range(4)]
    ho_pairs = [(z, below[1])] + [(above[t], below[t + 1]) for t in range(1, 4)]

    def project(t):
        for zz in ho_pairs[t]:
            PB[zz] = dot(HO[pl.ds(pl.multiple_of(zz * 128, 128), 128), :], WO[...]).astype(BF)
            sib_copy(zz).start()

    def rows16(index):
        return pl.ds(pl.multiple_of(index * 16, 16), 16)

    def chip_copy(t, d):
        kk = lax.rem(k + d, 8)
        return remote(
            RED.at[t, rows16(kk), :], RK.at[t, k], rk_s.at[t, d], rk_r.at[t, k], (c, 2 * kk + s)
        )

    def reduce_cores(t):
        for i, zz in enumerate(ho_pairs[t]):
            sib_copy(zz).wait_recv()
            own = PB[zz, pl.ds(pl.multiple_of(s * 64, 64), 64), :]
            RED[t, i * 64 : (i + 1) * 64, :] = (own.astype(F32) + SB[zz].astype(F32)).astype(BF)
        for d in range(1, 8):
            chip_copy(t, d).start()
        RK[t, k] = RED[t, rows16(k), :]

    quarter = lax.rem(k, 4)

    def turn_copy(t):
        za, zb = ho_pairs[t]
        target = jnp.where(k < 4, za, zb)
        return remote(
            TS.at[t], TR.at[rows16(quarter), :], t_s.at[t], t_r.at[quarter],
            (yl * 8 + target, 2 * z + s),
        )

    def reduce_chips(t):
        for d in range(1, 8):
            kk = lax.rem(k + d, 8)
            remote(TS.at[t], RK.at[t, kk], t_s.at[0], rk_r.at[t, kk], (c, e)).wait_recv()
        summed = RK[t, 0].astype(F32)
        for kk in range(1, 8):
            summed = summed + RK[t, kk].astype(F32)
        TS[t] = summed.astype(BF)
        if t > 0:
            turn_copy(t).start()
            return

        @pl.when(turn_self)
        def _():
            TR[rows16(quarter), :] = TS[t]

        @pl.when(jnp.logical_not(turn_self))
        def _():
            turn_copy(t).start()

    ho_arrive(below[1], True, True)
    project(0)
    ho_arrive(above[1], False, True)
    ho_arrive(below[2], True, True)
    project(1)
    reduce_cores(0)
    ho_arrive(above[2], False, True)
    ho_arrive(below[3], True, True)
    project(2)
    reduce_cores(1)
    reduce_chips(0)
    ho_arrive(above[3], False, False)
    ho_arrive(below[4], True, False)
    project(3)
    reduce_cores(2)
    reduce_chips(1)
    reduce_cores(3)
    reduce_chips(2)

    for which in range(2):
        own_weight(which).wait()

    def weight_share(kk, core):
        expert = 2 * kk + core
        return remote(W.at[expert], W.at[expert], wf_s.at[kk], wf_r.at[kk], (c, sib))

    def share_weights():
        weight_share(k, s).start()
        for d in range(1, 8):
            kk = lax.rem(k + d, 8)
            for which in range(2):
                piece = W.at[2 * kk + s, :, pl.ds(which * 128, 128)]
                remote(piece, piece, w_s.at[0, which], w_r.at[kk, which], (c, e)).wait_recv()
            weight_share(kk, s).start()

    reduce_chips(3)
    for d in range(1, 8):
        down_weight(d).start()

    for j in range(8):

        @pl.when(8 * s + j != e)
        def _():
            remote(HS.at[0], HR.at[j], hd_s.at[0], hd_r.at[j], (c, e)).wait_recv()

    fetch_router.wait()
    for q in range(4):

        @pl.when(jnp.logical_not((z == k) & (turn_base + q == k)))
        def _():
            remote(TS.at[0], TR.at[rows16(q), :], t_s.at[0], t_r.at[q], (c, e)).wait_recv()

    rows_in = HR[...].reshape(TOKENS, 1024)
    residual = (rows_in[:, 0:SL] + TR[...].astype(F32)).astype(BF).astype(F32)
    gains = gain[k]
    lane = iota((TOKENS, META), 1)
    logits = dot_t((residual * gains).astype(BF), RT[...])
    squares = jnp.sum(residual * residual, axis=1, keepdims=True)
    ST[k] = jnp.where(lane == EXPERTS, squares, logits)

    def stat_copy(d):
        kk = lax.rem(k + d, 8)
        return remote(ST.at[k], ST.at[k], st_s.at[d], st_r.at[k], (c, 2 * kk + s))

    for d in range(1, 8):
        stat_copy(d).start()
    for d in range(1, 8):
        kk = lax.rem(k + d, 8)
        remote(ST.at[kk], ST.at[kk], st_s.at[0], st_r.at[kk], (c, e)).wait_recv()
    stats = ST[0]
    for kk in range(1, 8):
        stats = stats + ST[kk]
    inverse = lax.rsqrt(column_of(stats, EXPERTS) / D + NORM_EPS)
    normed = (residual * inverse * gains).astype(BF)
    affinity = 1.0 / (1.0 + jnp.exp(-(stats * inverse)))
    routed = rows_in[:, SL:1024]
    route0, route1 = column_of(routed, 0), column_of(routed, 1)
    lane_f = lane.astype(F32)
    chosen0 = jnp.sum(jnp.where(lane_f == route0, affinity, 0.0), axis=1, keepdims=True)
    chosen1 = jnp.sum(jnp.where(lane_f == route1, affinity, 0.0), axis=1, keepdims=True)
    scale = ROUTE_SCALE / (chosen0 + chosen1)
    meta = jnp.where(lane == 0, route0, jnp.where(lane == 1, route1, 0.0))
    for index, weight in ((2, chosen0 * scale), (4, chosen1 * scale)):
        coarse = weight.astype(BF).astype(F32)
        meta = jnp.where(lane == index, coarse, meta)
        meta = jnp.where(lane == index + 1, weight - coarse, meta)

    def rows_of(cc):
        return pl.ds(pl.multiple_of(cc * TOKENS, TOKENS), TOKENS)

    X[rows_of(c), 0:SL] = normed
    X[rows_of(c), SL:1024] = meta.astype(BF)

    def row_copy(cc, way):
        block = X.at[rows_of(cc), :]
        target = {"y": c_y, "up": c_up, "down": c_down}[way]
        sems = {"y": xy_s, "up": xp_s, "down": xm_s}[way]
        return remote(block, block, sems.at[cc], x_r.at[cc], (target, e))

    row_copy(c, "up").start()
    row_copy(c, "down").start()
    row_copy(c, "y").start()
    row_copy(c_y, "y").wait_recv()

    @pl.when(s == 0)
    def _():
        row_copy(c_y, "up").start()
        row_copy(c_y, "down").start()

    def arrive(zz, way, go_on):
        own, other = yl * 8 + zz, (1 - yl) * 8 + zz
        row_copy(own, way).wait_recv()
        if go_on:
            row_copy(own, way).start()

        @pl.when(s == 1)
        def _():
            row_copy(own, "y").start()

        row_copy(other, way).wait_recv()
        if go_on:

            @pl.when(s == 0)
            def _():
                row_copy(other, way).start()

    chunks = [(z, near[1])] + [(far[t], near[t + 1]) for t in range(1, 4)]

    def places(t):
        za, zb = chunks[t]
        return [(0, za), (1, za), (0, zb), (1, zb)]

    def part(kk):
        return pl.ds(pl.multiple_of(kk * 32, 32), 32)

    def half_copy(t, d):
        kk = lax.rem(k + d, 8)
        return remote(
            GS.at[t, :, part(kk), :], GR.at[t, k], g_s.at[t, d], g_r.at[t, k], (c, 2 * kk + s)
        )

    def first_layers(t):
        for i, (y, zz) in enumerate(places(t)):
            XC[t, i * 64 : (i + 1) * 64, :] = X[rows_of(y * 8 + zz), :]
        acc0[...] = jnp.zeros(acc0.shape, F32)
        acc1[...] = jnp.zeros(acc1.shape, F32)
        routed_here = XC[t, :, SL:1024].astype(F32)
        r0, r1 = column_of(routed_here, 0), column_of(routed_here, 1)

        def one_expert(expert, carry):
            product = dot(XC[t, :, 0:SL], W[expert])
            number = expert.astype(F32)
            acc0[...] += jnp.where(r0 == number, product, 0.0)
            acc1[...] += jnp.where(r1 == number, product, 0.0)
            return carry

        lax.fori_loop(0, EXPERTS, one_expert, 0)
        GS[t, 0] = acc0[...].astype(BF)
        GS[t, 1] = acc1[...].astype(BF)
        for d in range(1, 8):
            half_copy(t, d).start()
        GR[t, k] = GS[t, :, part(k), :]

    def act_copy(t, d):
        kk = lax.rem(k + d, 8)
        block = A.at[t, :, part(k), :]
        return remote(block, block, a_s.at[t, d], a_r.at[t, k], (c, 2 * kk + s))

    def activate(t):
        for d in range(1, 8):
            kk = lax.rem(k + d, 8)
            remote(GR.at[t, k], GR.at[t, kk], g_s.at[t, 0], g_r.at[t, kk], (c, e)).wait_recv()
        here = XC[t, part(k), SL:1024].astype(F32)
        for r in range(2):
            both = GR[t, 0, r].astype(F32)
            for kk in range(1, 8):
                both = both + GR[t, kk, r].astype(F32)
            weight = column_of(here, 2 + 2 * r) + column_of(here, 3 + 2 * r)
            gate, up = both[:, 0:128], both[:, 128:256]
            A[t, r, part(k), :] = (gate / (1.0 + jnp.exp(-gate)) * up * weight).astype(BF)
        for d in range(1, 8):
            act_copy(t, d).start()

    def partner_copy(y, zz):
        return remote(DP.at[zz, y], YB.at[zz], yb_s.at[zz], yb_r.at[zz], (c_y, e))

    def second_layer(t):
        for d in range(1, 8):
            kk = lax.rem(k + d, 8)
            block = A.at[t, :, part(kk), :]
            remote(block, block, a_s.at[t, 0], a_r.at[t, kk], (c, e)).wait_recv()
        routed_here = XC[t, :, SL:1024].astype(F32)
        r0, r1 = column_of(routed_here, 0), column_of(routed_here, 1)
        a0, a1 = A[t, 0].astype(F32), A[t, 1].astype(F32)
        for expert in range(EXPERTS):
            picked = jnp.where(r0 == float(expert), a0, 0.0) + jnp.where(
                r1 == float(expert), a1, 0.0
            )
            AC[:, expert * 128 : (expert + 1) * 128] = picked.astype(BF)
        out = dot(AC[...], WD[...])
        for i, (y, zz) in enumerate(places(t)):
            DP[zz, y] = out[i * 64 : (i + 1) * 64, :].astype(BF)

        @pl.when(s == 1)
        def _():
            for zz in chunks[t]:
                partner_copy(1 - yl, zz).start()

    def down_share(kk, core):
        block = WD.at[down_rows(2 * kk + core), :]
        return remote(block, block, df_s.at[kk], df_r.at[kk], (c, sib))

    arrive(near[1], "up", True)
    arrive(far[1], "down", True)
    share_weights()
    arrive(near[2], "up", True)
    arrive(far[2], "down", True)
    for kk in range(8):
        weight_share(kk, 1 - s).wait_recv()
    first_layers(0)
    arrive(near[3], "up", True)
    arrive(far[3], "down", False)
    first_layers(1)
    arrive(near[4], "up", False)
    activate(0)
    first_layers(2)
    activate(1)
    own_down.wait()
    down_share(k, s).start()
    for d in range(1, 8):
        kk = lax.rem(k + d, 8)
        block = WD.at[down_rows(2 * kk + s), :]
        remote(block, block, d_s.at[0], d_r.at[kk], (c, e)).wait_recv()
        down_share(kk, s).start()
    first_layers(3)
    activate(2)
    for kk in range(8):
        down_share(kk, 1 - s).wait_recv()
    second_layer(0)
    second_layer(1)
    activate(3)

    routed_all = X[:, SL:1024].astype(F32)
    lane_all = iota(routed_all.shape, 1).astype(F32)
    named = jnp.where(lane_all == column_of(routed_all, 0), 1.0, 0.0) + jnp.where(
        lane_all == column_of(routed_all, 1), 1.0, 0.0
    )
    CS[...] = jnp.broadcast_to(jnp.sum(named, axis=0, keepdims=True), CS.shape)
    count_copy = remote(CS, CR, c_s.at[0], c_r.at[0], (c, sib))
    count_copy.start()

    second_layer(2)
    second_layer(3)

    def joins(y):
        return (s == 0) | (y == yl)

    def complete(zz):
        @pl.when(s == 1)
        def _():
            partner_copy(yl, zz).wait_recv()
            DP[zz, yl] = (DP[zz, yl].astype(F32) + YB[zz].astype(F32)).astype(BF)

    def up_copy(source, step, y):
        return remote(source, RP.at[step, y], p_s.at[step, y], p_r.at[step, y], (c_up, e))

    def down_copy(source, step, y):
        return remote(source, RM.at[step, y], m_s.at[step, y], m_r.at[step, y], (c_down, e))

    ups = [along(4 - t) for t in range(5)]
    downs = [along(t - 3) for t in range(4)]
    complete(ups[0])
    complete(downs[0])
    for y in range(2):

        @pl.when(joins(y))
        def _():
            up_copy(DP.at[ups[0], y], 0, y).start()
            down_copy(DP.at[downs[0], y], 0, y).start()

    for t in range(1, 4):
        complete(ups[t])
        complete(downs[t])
        for y in range(2):

            @pl.when(joins(y))
            def _():
                up_copy(SP.at[0, y], t - 1, y).wait_recv()
                SP[t - 1, y] = (
                    DP[ups[t], y].astype(F32) + RP[t - 1, y].astype(F32)
                ).astype(BF)
                up_copy(SP.at[t - 1, y], t, y).start()
                if t < 3:
                    down_copy(SM.at[0, y], t - 1, y).wait_recv()
                    SM[t - 1, y] = (
                        DP[downs[t], y].astype(F32) + RM[t - 1, y].astype(F32)
                    ).astype(BF)
                    down_copy(SM.at[t - 1, y], t, y).start()

    def final(y):
        down_copy(SM.at[0, 0], 2, y).wait_recv()
        up_copy(SP.at[0, 0], 3, y).wait_recv()
        return DP[z, y].astype(F32) + RP[3, y].astype(F32) + RM[2, y].astype(F32)

    y_copy = remote(YS, YR, y_s.at[0], y_r.at[0], (c_y, e))

    @pl.when(s == 0)
    def _():
        YS[...] = final(1 - yl).astype(BF)
        y_copy.start()

    OS[...] = final(yl) + residual

    @pl.when(s == 0)
    def _():
        y_copy.wait_recv()
        OS[...] += YR[...].astype(F32)

    def owner_copy(j):
        return remote(
            OS.at[pl.ds(j * 8, 8), :], OR.at[k], o_s.at[j], o_r.at[k], (c, 8 * s + j)
        )

    for j in range(8):

        @pl.when(8 * s + j != e)
        def _():
            owner_copy(j).start()

        @pl.when(8 * s + j == e)
        def _():
            OR[k] = OS[pl.ds(j * 8, 8), :]

    count_copy.wait_recv()
    counts = (CS[...] + CR[...])[0:1, 0:EXPERTS]
    load_out[...] = LOAD_DECAY * ema[...] + (1.0 - LOAD_DECAY) * counts / 256.0

    for zz in range(8):
        sib_copy(zz).wait_send()
        weight_share(zz, s).wait_send()
        down_share(zz, s).wait_send()

        @pl.when(2 * zz + e_half != e)
        def _():
            hidden_copy(zz).wait_send()

        @pl.when(s == 1)
        def _():
            partner_copy(1 - yl, zz).wait_send()

    for d in range(1, 8):
        proj_copy(d).wait_send()
        down_weight(d).wait_send()
        stat_copy(d).wait_send()
        for which in range(2):
            weight_copy(d, which).wait_send()
        for t in range(4):
            chip_copy(t, d).wait_send()
            half_copy(t, d).wait_send()
            act_copy(t, d).wait_send()
    proj_share(yl).wait_send()

    @pl.when(jnp.logical_not(turn_self))
    def _():
        turn_copy(0).wait_send()

    for t in range(1, 4):
        turn_copy(t).wait_send()
    for half in range(2):
        for t in range(4):
            ho_copy(below[t], half, True).wait_send()
        for t in range(3):
            ho_copy(above[t], half, False).wait_send()

    both_rows = (yl == 1) & (s == 1)
    for t in range(8):
        zz = lax.rem(z + t, 8)
        if t > 0:
            kv_share(yl, zz, s).wait_send()

        @pl.when(yl == 1)
        def _():
            kv_share(0, zz, s).wait_send()

        @pl.when((yl == 0) & ((s == 0) | (zz == z)))
        def _():
            kv_copy(0, zz, "y").wait_send()

        @pl.when((s == 1) | (zz == z))
        def _():
            row_copy(yl * 8 + zz, "y").wait_send()

    for t in range(4):
        kv_copy(yl, near[t], "up").wait_send()
        row_copy(yl * 8 + near[t], "up").wait_send()

        @pl.when(both_rows)
        def _():
            kv_copy(0, near[t], "up").wait_send()

        @pl.when(s == 0)
        def _():
            row_copy((1 - yl) * 8 + near[t], "up").wait_send()

    for t in range(3):
        kv_copy(yl, far[t], "down").wait_send()
        row_copy(yl * 8 + far[t], "down").wait_send()

        @pl.when(both_rows)
        def _():
            kv_copy(0, far[t], "down").wait_send()

        @pl.when(s == 0)
        def _():
            row_copy((1 - yl) * 8 + far[t], "down").wait_send()

    for y in range(2):

        @pl.when(joins(y))
        def _():
            up_copy(DP.at[ups[0], y], 0, y).wait_send()
            down_copy(DP.at[downs[0], y], 0, y).wait_send()
            for t in range(1, 4):
                up_copy(SP.at[t - 1, y], t, y).wait_send()
                if t < 3:
                    down_copy(SM.at[t - 1, y], t, y).wait_send()

    @pl.when(s == 0)
    def _():
        y_copy.wait_send()

    count_copy.wait_send()
    for j in range(8):

        @pl.when(8 * s + j != e)
        def _():
            owner_copy(j).wait_send()

    for kk in range(8):

        @pl.when(2 * kk + e_half != e)
        def _():
            remote(
                OS.at[pl.ds(0, 8), :], OR.at[kk], o_s.at[0], o_r.at[kk], (c, e)
            ).wait_recv()

        layer_out[:, kk * SL : (kk + 1) * SL] = OR[kk].astype(BF)


def in_vmem(count):
    return [pl.BlockSpec(memory_space=pltpu.VMEM)] * count


def anywhere(count):
    return [pl.BlockSpec(memory_space=pl.ANY)] * count


def dma(*shape):
    return pltpu.SemaphoreType.DMA(shape)


def shaped(shape, dtype):
    return jax.ShapeDtypeStruct(shape, dtype)


def params(number):
    return pltpu.CompilerParams(
        collective_id=number, has_side_effects=True, vmem_limit_bytes=VMEM_LIMIT
    )


def body(
    hidden, q_nope, q_rope, kv_latent, k_rope, key_up, value_up, out_proj, ffn_gain, router,
    w_gate, w_up, w_down, routes, load_ema,
):
    v = pltpu.VMEM
    layer_out, new_load = pl.pallas_call(
        layer_kernel,
        out_shape=(shaped((8, D), BF), shaped((1, EXPERTS), F32)),
        in_specs=in_vmem(10) + anywhere(5),
        out_specs=tuple(in_vmem(2)),
        scratch_shapes=[
            v((2048, 640), BF), v((512, 640), BF), v((512, 1), F32), v((512, 1), F32),
            v((512, 512), F32), v((1024, 512), BF), v((512, SL), BF), v((8, 128, SL), BF),
            v((8, 64, SL), BF), v((4, 128, SL), BF), v((4, 8, 16, SL), BF), v((4, 16, SL), BF),
            v((64, SL), BF), v((8, 8, 1024), F32), v((8, 8, 1024), F32),
            v((1024, 1024), BF), v((16, SL, 256), BF), v((128, SL), BF), v((8, 64, META), F32),
            v((4, 256, 1024), BF), v((256, 256), F32), v((256, 256), F32),
            v((4, 2, 256, 256), BF), v((4, 8, 2, 32, 256), BF), v((4, 2, 256, 128), BF),
            v((2048, SL), BF), v((256, 2048), BF), v((8, 2, 64, SL), BF), v((8, 64, SL), BF),
            v((4, 2, 64, SL), BF), v((3, 2, 64, SL), BF), v((3, 2, 64, SL), BF),
            v((2, 2, 64, SL), BF), v((64, SL), BF), v((64, SL), BF), v((64, SL), F32),
            v((8, 8, SL), F32), v((8, 128), F32), v((8, 128), F32),
            dma(5), dma(16), dma(16), dma(16), dma(16), dma(16), dma(16), dma(8), dma(8),
            dma(1), dma(1), dma(8), dma(8),
            dma(8, 2), dma(8, 2), dma(8), dma(8), dma(8, 2), dma(8, 2), dma(8, 2), dma(8), dma(8),
            dma(4, 8), dma(4, 8), dma(4), dma(4),
            dma(8), dma(8), dma(8), dma(8), dma(8), dma(8), dma(16), dma(16), dma(16), dma(16),
            dma(4, 8), dma(4, 8), dma(4, 8), dma(4, 8),
            dma(8), dma(8), dma(4, 2), dma(4, 2), dma(3, 2), dma(3, 2), dma(1), dma(1), dma(8),
            dma(8), dma(1), dma(1),
        ],
        compiler_params=params(0),
        name="layer",
    )(
        q_nope, q_rope, kv_latent, k_rope.T, key_up, value_up, hidden, routes.T,
        ffn_gain.reshape(8, 1, SL), load_ema.reshape(1, EXPERTS), out_proj, router.T, w_gate, w_up, w_down,
    )
    return layer_out, new_load.reshape(EXPERTS)


def solution(mesh):
    placed = (
        P(("ctx", "ep"), None),
        P("ctx", "ep"),
        P("ctx", "ep"),
        P("ctx", None),
        P("ctx", None),
        P(None, "ep"),
        P(None, "ep"),
        P(("ep", "ctx"), None),
        P(),
        P(),
        P("ep", None, "ctx"),
        P("ep", None, "ctx"),
        P("ep", "ctx", None),
        P(("ctx", "ep"), None),
        P(),
    )
    return jax.shard_map(
        body, mesh=mesh, in_specs=placed, out_specs=(P(("ctx", "ep"), None), P()), check_vma=False
    )
```

time: 546 us -> 234 us (0.43)
  waiting for transfers between devices: 288 us -> 0 us
  Pallas kernels: 0 us -> 230 us
  blocking collectives: 185 us -> 0 us
  matrix products: 40.6 us -> 0 us
  between operations: 14.6 us -> 0.65 us
    pallas_call x0 -> x1, Pallas kernels: none -> 230 us  [body(): pl.pallas_call(layer_kernel, out_shape=(shaped((8, D), BF), shaped((1, EX...]
    all_gather x3 -> x0, waiting for transfers between devices: 204 us -> none  [the longest x1 87.9 us: body(): slot_rows = lax.all_gather(arrived, 'ctx', axis=0, tiled=True)]
    psum x1 -> x0, blocking collectives: 135 us -> none  [body(): total_load = lax.psum(local_load, ('ctx', 'ep'))]
    reduce_scatter x2 -> x0, waiting for transfers between devices: 72.6 us -> none  [the longest x1 72.6 us: body(): lax.psum_scatter(projected.astype(jnp.bfloat16), 'ep', scatter_dimension=...]
    dot_general x10 -> x0, matrix products: 40.6 us -> none  [the longest x1 15.3 us: body(): jnp.dot(activations, down_proj, preferred_element_type=jnp.float32)]
    all_gather x1 -> x0, blocking collectives: 33 us -> none  [attend_all(): rope_piece = lax.all_gather(k_rope, 'ctx', axis=0, tiled=True)]
    all_to_all x1 -> x0, blocking collectives: 17.4 us -> none  [body(): lax.all_to_all(outgoing, 'ep', split_axis=0, concat_axis=0, tiled=True)]
    all_to_all x1 -> x0, waiting for transfers between devices: 9.23 us -> none  [body(): lax.all_to_all(summed.reshape(expert_count, capacity, D), 'ep', split_axi...]
  transfers between devices with their start and end apart: 6 -> 0, of which waited for: 5 -> 0; matrix products, arithmetic and copies ran while one was open for 4% -> 0% of each run, Pallas kernels for 0% -> 0%
where the time goes in v2:
time: 234 us; the launch traced here: 233 us
  Pallas kernels  230 us (98%)
  local copies, waits for them, and re-layouts  2.66 us (1%)
    pallas_call x1, Pallas kernels, body(): pl.pallas_call(layer_kernel, out_shape=(shaped((8, D), BF), shaped((1, EX...  230 us

profile of v2, /device:TPU:1, one launch (start us, length us, event | category | flops | bytes accessed | tf_op | source)
XLA Modules:
  0.0 233.4 jit_solution(6327699492182970568)
XLA Ops:
  0.6 230.1 %layer.1 = (bf16[8,7168]{1,0:T(8,128)(2,1)}, f32[1,16]{1,0:T(1,128)}) custom-call(bf16[128,512]{1,0:T(8,128)(2,1)} %q_nope.1, bf16[128,256]{1,0:T(8,128)(2,1)} %q_rope.1, bf16[128,512]{1,0:T(8,128)(2,1)} %kv.1, bf16[64,128]{1,0:T(8,128)(2,1)} %bitcast.8, bf16[512,512]{1,0:T(8,128)(2,1)} %key_up.1, bf16[512,512]{1,0:T(8,128)(2,1)} %value_up.1, ...), custom_call_target="tpu_custom_call" | custom-call | tf_op jit(solution)/shard_map/layer/pallas_call | solution.py:900
  230.8 1.6 copy.19
  232.3 1.1 copy.20

commit v3 on v2

--- a/solution.py
+++ b/solution.py
@@ -65,11 +65,11 @@
     q_nope, q_rope, kv, k_rope, key_up, value_up, hidden, routes, gain, ema, out_proj, router, w_gate, w_up, w_down,
     layer_out, load_out,
     KV, Q, top, total, accum, HO, WO, PB, SB, RED, RK, TS, TR, HS, HR,
-    X, W, RT, ST, XC, acc0, acc1, GS, GR, A, WD, AC, DP, YB, RP, RM, SP, SM, YS, YR, OS, OR, CS, CR,
+    X, W, RT, ST, XC, acc0, acc1, GS, GR, A, WD, AC, DP, YB, RP, RM, SP, SM, YS, YR, OS, OR, CS, CR, MS, MR,
     local, kp_s, km_s, ky_s, kv_r, kf_s, kf_r, op_s, op_r, oy_s, oy_r, hd_s, hd_r,
     w_s, w_r, wf_s, wf_r, hp_s, hm_s, ho_r, sb_s, sb_r, rk_s, rk_r, t_s, t_r,
     st_s, st_r, d_s, d_r, df_s, df_r, xp_s, xm_s, xy_s, x_r, g_s, g_r, a_s, a_r,
-    yb_s, yb_r, p_s, p_r, m_s, m_r, y_s, y_r, o_s, o_r, c_s, c_r,
+    yb_s, yb_r, p_s, p_r, m_s, m_r, y_s, y_r, o_s, o_r, c_s, c_r, ms_s, ms_r,
 ):
     c, e, yl, z, k, s = place()
     sib = 2 * k + 1 - s
@@ -134,7 +134,19 @@
         def _():
             greet((yl * 8 + k, 2 * (turn_base + q) + s))
 
-    pl.semaphore_wait(barrier, 27 - turn_self.astype(jnp.int32))
+    scale_row = lax.rem(lax.div(k, 2), 2)
+
+    def scale_source(t):
+        return scale_row * 8 + jnp.where(k < 4, along(t), along(-1 - t))
+
+    for t in range(4):
+
+        @pl.when(scale_source(t) != c)
+        def _():
+            greet((scale_source(t), e))
+
+    scale_sends = jnp.where(yl == scale_row, jnp.where(k < 4, 7, 8), 0)
+    pl.semaphore_wait(barrier, 27 - turn_self.astype(jnp.int32) + scale_sends)
 
     def kv_copy(y, zz, way):
         block = KV.at[kv_rows(kv_slot(y, zz), s * 64, 64), :]
@@ -252,35 +264,32 @@
         kv_copy(0, z, "y").wait_recv()
         kv_share(0, z, s).start()
 
-        @pl.when(s == 1)
-        def _():
-            kv_copy(0, z, "up").start()
-            kv_copy(0, z, "down").start()
+        kv_copy(0, z, "up").start()
+        kv_copy(0, z, "down").start()
 
     def kv_arrive(zz, way, go_on):
         kv_copy(yl, zz, way).wait_recv()
-        if go_on:
+
+        @pl.when(go_on)
+        def _():
             kv_copy(yl, zz, way).start()
+
         kv_share(yl, zz, s).start()
-
-        @pl.when((yl == 0) & (s == 0))
-        def _():
-            kv_copy(0, zz, "y").start()
 
         @pl.when(yl == 1)
         def _():
             kv_copy(0, zz, way).wait_recv()
             kv_share(0, zz, s).start()
-            if go_on:
-
-                @pl.when(s == 1)
-                def _():
-                    kv_copy(0, zz, way).start()
+
+            @pl.when(go_on)
+            def _():
+                kv_copy(0, zz, way).start()
 
     score_scale = (NOPE + ROPE) ** (-0.5)
 
-    def attend(zz, own):
-        if not own:
+    def attend(zz, shared):
+        @pl.when(shared)
+        def _():
             kv_share(yl, zz, 1 - s).wait_recv()
 
         @pl.when(yl == 1)
@@ -307,29 +316,43 @@
         piece = WO.at[pl.ds(pl.multiple_of((yl * 8 + zz) * 32, 32), 32), :]
         return remote(out_proj.at[:, pl.ds(0, SL)], piece, op_s.at[0], op_r.at[zz], (c, e))
 
-    def proj_share(y):
-        row = WO.at[pl.ds(pl.multiple_of(y * 256, 256), 256), :]
-        return remote(row, row, oy_s.at[0], oy_r.at[0], (c_y, e))
-
-    kv_arrive(near[1], "up", True)
-    kv_arrive(far[1], "down", True)
-    attend(z, True)
-    kv_arrive(near[2], "up", True)
-    kv_arrive(far[2], "down", True)
-    attend(near[1], False)
-    attend(far[1], False)
-    kv_arrive(near[3], "up", True)
-    kv_arrive(far[3], "down", False)
-    attend(near[2], False)
-    attend(far[2], False)
-    kv_arrive(near[4], "up", False)
+    def proj_share(y, zz):
+        row = WO.at[pl.ds(pl.multiple_of((y * 8 + zz) * 32, 32), 32), :]
+        return remote(row, row, oy_s.at[zz], oy_r.at[zz], (c_y, e))
+
     own_proj.wait()
-    for d in range(1, 8):
-        proj_piece(lax.rem(z + d, 8)).wait_recv()
-    proj_share(yl).start()
-    attend(near[3], False)
-    attend(far[3], False)
-    attend(near[4], False)
+    proj_share(yl, z).start()
+
+    def attention_step(m, carry):
+        @pl.when(m < 5)
+        def _():
+            kv_arrive(along(-m), "up", m < 4)
+
+        @pl.when(m < 4)
+        def _():
+            kv_arrive(along(m), "down", m < 3)
+
+        @pl.when(m < 5)
+        def _():
+            proj_piece(along(-m)).wait_recv()
+            proj_share(yl, along(-m)).start()
+
+        @pl.when(m < 4)
+        def _():
+            proj_piece(along(m)).wait_recv()
+            proj_share(yl, along(m)).start()
+
+        def side(j, carry):
+            @pl.when((j == 0) | ((m > 1) & (m < 5)))
+            def _():
+                attend(along((2 * j - 1) * (m - 1)), m > 1)
+
+            return carry
+
+        lax.fori_loop(0, 2, side, 0)
+        return carry
+
+    lax.fori_loop(1, 6, attention_step, 0)
 
     own_rows = pl.ds(pl.multiple_of(z * 128, 128), 128)
     for h in range(HEAD_DEV):
@@ -347,12 +370,15 @@
     for half in range(2):
         ho_copy(z, half, True).start()
         ho_copy(z, half, False).start()
-    proj_share(1 - yl).wait_recv()
+    for zz in range(8):
+        proj_share(1 - yl, zz).wait_recv()
 
     def ho_arrive(zz, up, go_on):
         for half in range(2):
             ho_copy(zz, half, up).wait_recv()
-            if go_on:
+
+            @pl.when(go_on)
+            def _():
                 ho_copy(zz, half, up).start()
 
     def sib_copy(zz):
@@ -366,12 +392,19 @@
 
     below = [lax.rem(z + 8 - t, 8) for t in range(5)]
     above = [lax.rem(z + t, 8) for t in range(4)]
-    ho_pairs = [(z, below[1])] + [(above[t], below[t + 1]) for t in range(1, 4)]
+
+    def ho_pair(t):
+        return lax.rem(z + t, 8), lax.rem(z + 7 - t, 8)
 
     def project(t):
-        for zz in ho_pairs[t]:
+        def one(j, carry):
+            za, zb = ho_pair(t)
+            zz = jnp.where(j == 0, za, zb)
             PB[zz] = dot(HO[pl.ds(pl.multiple_of(zz * 128, 128), 128), :], WO[...]).astype(BF)
             sib_copy(zz).start()
+            return carry
+
+        lax.fori_loop(0, 2, one, 0)
 
     def rows16(index):
         return pl.ds(pl.multiple_of(index * 16, 16), 16)
@@ -383,7 +416,7 @@
         )
 
     def reduce_cores(t):
-        for i, zz in enumerate(ho_pairs[t]):
+        for i, zz in enumerate(ho_pair(t)):
             sib_copy(zz).wait_recv()
             own = PB[zz, pl.ds(pl.multiple_of(s * 64, 64), 64), :]
             RED[t, i * 64 : (i + 1) * 64, :] = (own.astype(F32) + SB[zz].astype(F32)).astype(BF)
@@ -394,7 +427,7 @@
     quarter = lax.rem(k, 4)
 
     def turn_copy(t):
-        za, zb = ho_pairs[t]
+        za, zb = ho_pair(t)
         target = jnp.where(k < 4, za, zb)
         return remote(
             TS.at[t], TR.at[rows16(quarter), :], t_s.at[t], t_r.at[quarter],
@@ -409,56 +442,58 @@
         for kk in range(1, 8):
             summed = summed + RK[t, kk].astype(F32)
         TS[t] = summed.astype(BF)
-        if t > 0:
+        home = turn_self & (t == 0)
+
+        @pl.when(home)
+        def _():
+            TR[rows16(quarter), :] = TS[t]
+
+        @pl.when(jnp.logical_not(home))
+        def _():
             turn_copy(t).start()
-            return
-
-        @pl.when(turn_self)
-        def _():
-            TR[rows16(quarter), :] = TS[t]
-
-        @pl.when(jnp.logical_not(turn_self))
-        def _():
-            turn_copy(t).start()
-
-    ho_arrive(below[1], True, True)
-    project(0)
-    ho_arrive(above[1], False, True)
-    ho_arrive(below[2], True, True)
-    project(1)
-    reduce_cores(0)
-    ho_arrive(above[2], False, True)
-    ho_arrive(below[3], True, True)
-    project(2)
-    reduce_cores(1)
-    reduce_chips(0)
-    ho_arrive(above[3], False, False)
-    ho_arrive(below[4], True, False)
-    project(3)
-    reduce_cores(2)
-    reduce_chips(1)
-    reduce_cores(3)
-    reduce_chips(2)
-
-    for which in range(2):
-        own_weight(which).wait()
+
+    def down_rows_of(d):
+        return WD.at[down_rows(2 * lax.rem(k + d, 8) + s), :]
 
     def weight_share(kk, core):
         expert = 2 * kk + core
         return remote(W.at[expert], W.at[expert], wf_s.at[kk], wf_r.at[kk], (c, sib))
 
-    def share_weights():
-        weight_share(k, s).start()
-        for d in range(1, 8):
-            kk = lax.rem(k + d, 8)
-            for which in range(2):
-                piece = W.at[2 * kk + s, :, pl.ds(which * 128, 128)]
-                remote(piece, piece, w_s.at[0, which], w_r.at[kk, which], (c, e)).wait_recv()
-            weight_share(kk, s).start()
-
-    reduce_chips(3)
-    for d in range(1, 8):
-        down_weight(d).start()
+    def share_weight(d):
+        kk = lax.rem(k + d, 8)
+        for which in range(2):
+            piece = W.at[2 * kk + s, :, pl.ds(which * 128, 128)]
+            remote(piece, piece, w_s.at[0, which], w_r.at[kk, which], (c, e)).wait_recv()
+        weight_share(kk, s).start()
+
+    for which in range(2):
+        own_weight(which).wait()
+    weight_share(k, s).start()
+
+    def head_step(t, carry):
+        @pl.when(t < 4)
+        def _():
+            za, zb = ho_pair(t)
+
+            @pl.when(t > 0)
+            def _():
+                ho_arrive(za, False, t < 3)
+
+            ho_arrive(zb, True, t < 3)
+            project(t)
+
+        @pl.when((t > 0) & (t < 5))
+        def _():
+            reduce_cores(t - 1)
+
+        @pl.when(t > 1)
+        def _():
+            reduce_chips(t - 2)
+
+        share_weight(t + 1)
+        return carry
+
+    lax.fori_loop(0, 6, head_step, 0)
 
     for j in range(8):
 
@@ -477,7 +512,8 @@
     residual = (rows_in[:, 0:SL] + TR[...].astype(F32)).astype(BF).astype(F32)
     gains = gain[k]
     lane = iota((TOKENS, META), 1)
-    logits = dot_t((residual * gains).astype(BF), RT[...])
+    scaled = (residual * gains).astype(BF)
+    logits = dot_t(scaled, RT[...])
     squares = jnp.sum(residual * residual, axis=1, keepdims=True)
     ST[k] = jnp.where(lane == EXPERTS, squares, logits)
 
@@ -487,6 +523,25 @@
 
     for d in range(1, 8):
         stat_copy(d).start()
+    routed = rows_in[:, SL:1024]
+    route0, route1 = column_of(routed, 0), column_of(routed, 1)
+
+    def rows_of(cc):
+        return pl.ds(pl.multiple_of(cc * TOKENS, TOKENS), TOKENS)
+
+    X[rows_of(c), 0:SL] = scaled
+    X[rows_of(c), SL:1024] = routed.astype(BF)
+
+    def row_copy(cc, way):
+        block = X.at[rows_of(cc), :]
+        target = {"y": c_y, "up": c_up, "down": c_down}[way]
+        sems = {"y": xy_s, "up": xp_s, "down": xm_s}[way]
+        return remote(block, block, sems.at[cc], x_r.at[cc], (target, e))
+
+    row_copy(c, "up").start()
+    row_copy(c, "down").start()
+    row_copy(c, "y").start()
+
     for d in range(1, 8):
         kk = lax.rem(k + d, 8)
         remote(ST.at[kk], ST.at[kk], st_s.at[0], st_r.at[kk], (c, e)).wait_recv()
@@ -494,63 +549,63 @@
     for kk in range(1, 8):
         stats = stats + ST[kk]
     inverse = lax.rsqrt(column_of(stats, EXPERTS) / D + NORM_EPS)
-    normed = (residual * inverse * gains).astype(BF)
     affinity = 1.0 / (1.0 + jnp.exp(-(stats * inverse)))
-    routed = rows_in[:, SL:1024]
-    route0, route1 = column_of(routed, 0), column_of(routed, 1)
     lane_f = lane.astype(F32)
     chosen0 = jnp.sum(jnp.where(lane_f == route0, affinity, 0.0), axis=1, keepdims=True)
     chosen1 = jnp.sum(jnp.where(lane_f == route1, affinity, 0.0), axis=1, keepdims=True)
     scale = ROUTE_SCALE / (chosen0 + chosen1)
-    meta = jnp.where(lane == 0, route0, jnp.where(lane == 1, route1, 0.0))
-    for index, weight in ((2, chosen0 * scale), (4, chosen1 * scale)):
-        coarse = weight.astype(BF).astype(F32)
-        meta = jnp.where(lane == index, coarse, meta)
-        meta = jnp.where(lane == index + 1, weight - coarse, meta)
-
-    def rows_of(cc):
-        return pl.ds(pl.multiple_of(cc * TOKENS, TOKENS), TOKENS)
-
-    X[rows_of(c), 0:SL] = normed
-    X[rows_of(c), SL:1024] = meta.astype(BF)
-
-    def row_copy(cc, way):
-        block = X.at[rows_of(cc), :]
-        target = {"y": c_y, "up": c_up, "down": c_down}[way]
-        sems = {"y": xy_s, "up": xp_s, "down": xm_s}[way]
-        return remote(block, block, sems.at[cc], x_r.at[cc], (target, e))
-
-    row_copy(c, "up").start()
-    row_copy(c, "down").start()
-    row_copy(c, "y").start()
+    MS[...] = jnp.where(
+        lane == 0, chosen0 * scale, jnp.where(lane == 1, chosen1 * scale, inverse)
+    )
+    scale_half = lax.rem(k, 2)
+
+    def scale_copy(y, t):
+        target = jnp.where(k < 4, along(-t), along(1 + t))
+        return remote(
+            MS.at[pl.ds(pl.multiple_of(scale_half * 32, 32), 32), :], MR.at[t], ms_s.at[y, t],
+            ms_r.at[t], (y * 8 + target, e),
+        )
+
+    def scale_stays(y, t):
+        return (k < 4) & (t == 0) & (y == yl)
+
+    @pl.when(yl == scale_row)
+    def _():
+        for t in range(4):
+            for y in range(2):
+
+                @pl.when(jnp.logical_not(scale_stays(y, t)))
+                def _():
+                    scale_copy(y, t).start()
+
+                @pl.when(scale_stays(y, t))
+                def _():
+                    MR[t] = MS[pl.ds(pl.multiple_of(scale_half * 32, 32), 32), :]
+
     row_copy(c_y, "y").wait_recv()
 
-    @pl.when(s == 0)
-    def _():
-        row_copy(c_y, "up").start()
-        row_copy(c_y, "down").start()
+    row_copy(c_y, "up").start()
+    row_copy(c_y, "down").start()
 
     def arrive(zz, way, go_on):
         own, other = yl * 8 + zz, (1 - yl) * 8 + zz
         row_copy(own, way).wait_recv()
-        if go_on:
+
+        @pl.when(go_on)
+        def _():
             row_copy(own, way).start()
 
-        @pl.when(s == 1)
-        def _():
-            row_copy(own, "y").start()
-
         row_copy(other, way).wait_recv()
-        if go_on:
-
-            @pl.when(s == 0)
-            def _():
-                row_copy(other, way).start()
-
-    chunks = [(z, near[1])] + [(far[t], near[t + 1]) for t in range(1, 4)]
+
+        @pl.when(go_on)
+        def _():
+            row_copy(other, way).start()
+
+    def chunk(t):
+        return along(t), along(-1 - t)
 
     def places(t):
-        za, zb = chunks[t]
+        za, zb = chunk(t)
         return [(0, za), (1, za), (0, zb), (1, zb)]
 
     def part(kk):
@@ -593,12 +648,18 @@
         for d in range(1, 8):
             kk = lax.rem(k + d, 8)
             remote(GR.at[t, k], GR.at[t, kk], g_s.at[t, 0], g_r.at[t, kk], (c, e)).wait_recv()
-        here = XC[t, part(k), SL:1024].astype(F32)
+        @pl.when(scale_source(t) != c)
+        def _():
+            remote(MR.at[t], MR.at[t], ms_s.at[0, 0], ms_r.at[t], (c, e)).wait_recv()
+
+        here = MR[t]
+        inverse_here = column_of(here, 2)
         for r in range(2):
             both = GR[t, 0, r].astype(F32)
             for kk in range(1, 8):
                 both = both + GR[t, kk, r].astype(F32)
-            weight = column_of(here, 2 + 2 * r) + column_of(here, 3 + 2 * r)
+            both = both * inverse_here
+            weight = column_of(here, r)
             gate, up = both[:, 0:128], both[:, 128:256]
             A[t, r, part(k), :] = (gate / (1.0 + jnp.exp(-gate)) * up * weight).astype(BF)
         for d in range(1, 8):
@@ -626,7 +687,7 @@
 
         @pl.when(s == 1)
         def _():
-            for zz in chunks[t]:
+            for zz in chunk(t):
                 partner_copy(1 - yl, zz).start()
 
     def down_share(kk, core):
@@ -634,34 +695,51 @@
         return remote(block, block, df_s.at[kk], df_r.at[kk], (c, sib))
 
     arrive(near[1], "up", True)
-    arrive(far[1], "down", True)
-    share_weights()
-    arrive(near[2], "up", True)
-    arrive(far[2], "down", True)
-    for kk in range(8):
-        weight_share(kk, 1 - s).wait_recv()
-    first_layers(0)
-    arrive(near[3], "up", True)
-    arrive(far[3], "down", False)
-    first_layers(1)
-    arrive(near[4], "up", False)
-    activate(0)
-    first_layers(2)
-    activate(1)
-    own_down.wait()
-    down_share(k, s).start()
-    for d in range(1, 8):
-        kk = lax.rem(k + d, 8)
-        block = WD.at[down_rows(2 * kk + s), :]
-        remote(block, block, d_s.at[0], d_r.at[kk], (c, e)).wait_recv()
-        down_share(kk, s).start()
-    first_layers(3)
-    activate(2)
-    for kk in range(8):
-        down_share(kk, 1 - s).wait_recv()
-    second_layer(0)
-    second_layer(1)
-    activate(3)
+    share_weight(7)
+
+    def layer_step(t, carry):
+        @pl.when(t < 3)
+        def _():
+            arrive(along(t + 1), "down", t < 2)
+            arrive(along(-2 - t), "up", t < 2)
+
+        @pl.when(t == 0)
+        def _():
+            for kk in range(8):
+                weight_share(kk, 1 - s).wait_recv()
+            for d in range(1, 8):
+                down_weight(d).start()
+
+        @pl.when(t < 4)
+        def _():
+            first_layers(t)
+
+        @pl.when(t == 1)
+        def _():
+            own_down.wait()
+            down_share(k, s).start()
+            for d in range(1, 8):
+                block = down_rows_of(d)
+                kk = lax.rem(k + d, 8)
+                remote(block, block, d_s.at[0], d_r.at[kk], (c, e)).wait_recv()
+                down_share(kk, s).start()
+
+        @pl.when((t > 0) & (t < 5))
+        def _():
+            activate(t - 1)
+
+        @pl.when(t == 2)
+        def _():
+            for kk in range(8):
+                down_share(kk, 1 - s).wait_recv()
+
+        @pl.when(t > 1)
+        def _():
+            second_layer(t - 2)
+
+        return carry
+
+    lax.fori_loop(0, 6, layer_step, 0)
 
     routed_all = X[:, SL:1024].astype(F32)
     lane_all = iota(routed_all.shape, 1).astype(F32)
@@ -671,9 +749,6 @@
     CS[...] = jnp.broadcast_to(jnp.sum(named, axis=0, keepdims=True), CS.shape)
     count_copy = remote(CS, CR, c_s.at[0], c_r.at[0], (c, sib))
     count_copy.start()
-
-    second_layer(2)
-    second_layer(3)
 
     def joins(y):
         return (s == 0) | (y == yl)
@@ -781,7 +856,8 @@
             chip_copy(t, d).wait_send()
             half_copy(t, d).wait_send()
             act_copy(t, d).wait_send()
-    proj_share(yl).wait_send()
+    for zz in range(8):
+        proj_share(yl, zz).wait_send()
 
     @pl.when(jnp.logical_not(turn_self))
     def _():
@@ -795,7 +871,7 @@
         for t in range(3):
             ho_copy(above[t], half, False).wait_send()
 
-    both_rows = (yl == 1) & (s == 1)
+    both_rows = yl == 1
     for t in range(8):
         zz = lax.rem(z + t, 8)
         if t > 0:
@@ -805,11 +881,11 @@
         def _():
             kv_share(0, zz, s).wait_send()
 
-        @pl.when((yl == 0) & ((s == 0) | (zz == z)))
+        @pl.when((yl == 0) & (zz == z))
         def _():
             kv_copy(0, zz, "y").wait_send()
 
-        @pl.when((s == 1) | (zz == z))
+        @pl.when(zz == z)
         def _():
             row_copy(yl * 8 + zz, "y").wait_send()
 
@@ -821,9 +897,7 @@
         def _():
             kv_copy(0, near[t], "up").wait_send()
 
-        @pl.when(s == 0)
-        def _():
-            row_copy((1 - yl) * 8 + near[t], "up").wait_send()
+        row_copy((1 - yl) * 8 + near[t], "up").wait_send()
 
     for t in range(3):
         kv_copy(yl, far[t], "down").wait_send()
@@ -833,9 +907,7 @@
         def _():
             kv_copy(0, far[t], "down").wait_send()
 
-        @pl.when(s == 0)
-        def _():
-            row_copy((1 - yl) * 8 + far[t], "down").wait_send()
+        row_copy((1 - yl) * 8 + far[t], "down").wait_send()
 
     for y in range(2):
 
@@ -853,6 +925,16 @@
         y_copy.wait_send()
 
     count_copy.wait_send()
+
+    @pl.when(yl == scale_row)
+    def _():
+        for t in range(4):
+            for y in range(2):
+
+                @pl.when(jnp.logical_not(scale_stays(y, t)))
+                def _():
+                    scale_copy(y, t).wait_send()
+
     for j in range(8):
 
         @pl.when(8 * s + j != e)
@@ -913,15 +995,16 @@
             v((2048, SL), BF), v((256, 2048), BF), v((8, 2, 64, SL), BF), v((8, 64, SL), BF),
             v((4, 2, 64, SL), BF), v((3, 2, 64, SL), BF), v((3, 2, 64, SL), BF),
             v((2, 2, 64, SL), BF), v((64, SL), BF), v((64, SL), BF), v((64, SL), F32),
-            v((8, 8, SL), F32), v((8, 128), F32), v((8, 128), F32),
+            v((8, 8, SL), F32), v((8, 128), F32), v((8, 128), F32), v((64, META), F32),
+            v((4, 32, META), F32),
             dma(5), dma(16), dma(16), dma(16), dma(16), dma(16), dma(16), dma(8), dma(8),
-            dma(1), dma(1), dma(8), dma(8),
+            dma(8), dma(8), dma(8), dma(8),
             dma(8, 2), dma(8, 2), dma(8), dma(8), dma(8, 2), dma(8, 2), dma(8, 2), dma(8), dma(8),
             dma(4, 8), dma(4, 8), dma(4), dma(4),
             dma(8), dma(8), dma(8), dma(8), dma(8), dma(8), dma(16), dma(16), dma(16), dma(16),
             dma(4, 8), dma(4, 8), dma(4, 8), dma(4, 8),
             dma(8), dma(8), dma(4, 2), dma(4, 2), dma(3, 2), dma(3, 2), dma(1), dma(1), dma(8),
-            dma(8), dma(1), dma(1),
+            dma(8), dma(1), dma(1), dma(2, 4), dma(4),
         ],
         compiler_params=params(0),
         name="layer",

time: 234 us -> 210 us (0.90)
  Pallas kernels: 230 us -> 206 us
    pallas_call x1, Pallas kernels: 230 us -> 206 us  [body(): pl.pallas_call(layer_kernel, out_shape=(shaped((8, D), BF), shaped((1, EX...]
where the time goes in v3:
time: 210 us; the launch traced here: 209 us
  Pallas kernels  206 us (98%)
  local copies, waits for them, and re-layouts  2.66 us (1%)
    pallas_call x1, Pallas kernels, body(): pl.pallas_call(layer_kernel, out_shape=(shaped((8, D), BF), shaped((1, EX...  206 us

profile of v3, /device:TPU:1, one launch (start us, length us, event | category | flops | bytes accessed | tf_op | source)
XLA Modules:
  0.0 209.3 jit_solution(1307822490780508153)
XLA Ops:
  0.6 206.0 %layer.1 = (bf16[8,7168]{1,0:T(8,128)(2,1)}, f32[1,16]{1,0:T(1,128)}) custom-call(bf16[128,512]{1,0:T(8,128)(2,1)} %q_nope.1, bf16[128,256]{1,0:T(8,128)(2,1)} %q_rope.1, bf16[128,512]{1,0:T(8,128)(2,1)} %kv.1, bf16[64,128]{1,0:T(8,128)(2,1)} %bitcast.8, bf16[512,512]{1,0:T(8,128)(2,1)} %key_up.1, bf16[512,512]{1,0:T(8,128)(2,1)} %value_up.1, ...), custom_call_target="tpu_custom_call" | custom-call | tf_op jit(solution)/shard_map/layer/pallas_call | solution.py:982
  206.6 1.6 copy.19
  208.2 1.1 copy.20

commit v4 on v3

--- a/solution.py
+++ b/solution.py
@@ -222,7 +222,7 @@
 
     for which in range(2):
         own_weight(which).start()
-    for d in range(1, 8):
+    for d in (4, 3, 5, 2, 6, 1, 7):
         for which in range(2):
             weight_copy(d, which).start()
     RT[...] = jnp.zeros(RT.shape, BF)
@@ -714,7 +714,11 @@
         def _():
             first_layers(t)
 
-        @pl.when(t == 1)
+        @pl.when((t > 0) & (t < 5))
+        def _():
+            activate(t - 1)
+
+        @pl.when(t == 3)
         def _():
             own_down.wait()
             down_share(k, s).start()
@@ -724,22 +728,18 @@
                 remote(block, block, d_s.at[0], d_r.at[kk], (c, e)).wait_recv()
                 down_share(kk, s).start()
 
-        @pl.when((t > 0) & (t < 5))
-        def _():
-            activate(t - 1)
-
-        @pl.when(t == 2)
+        @pl.when(t == 4)
         def _():
             for kk in range(8):
                 down_share(kk, 1 - s).wait_recv()
 
-        @pl.when(t > 1)
-        def _():
-            second_layer(t - 2)
+        @pl.when(t > 3)
+        def _():
+            second_layer(t - 4)
 
         return carry
 
-    lax.fori_loop(0, 6, layer_step, 0)
+    lax.fori_loop(0, 8, layer_step, 0)
 
     routed_all = X[:, SL:1024].astype(F32)
     lane_all = iota(routed_all.shape, 1).astype(F32)

time: 210 us -> 208 us (level)
  no operation moved by 1% of the time
where the time goes in v4:
time: 208 us
  Pallas kernels  205 us (99%)
  local copies, waits for them, and re-layouts  2.66 us (1%)
    pallas_call x1, Pallas kernels, body(): pl.pallas_call(layer_kernel, out_shape=(shaped((8, D), BF), shaped((1, EX...  205 us

profile of v4, /device:TPU:1, one launch (start us, length us, event | category | flops | bytes accessed | tf_op | source)
XLA Modules:
  0.0 208.3 jit_solution(7939035107247579843)
XLA Ops:
  0.6 205.0 %layer.1 = (bf16[8,7168]{1,0:T(8,128)(2,1)}, f32[1,16]{1,0:T(1,128)}) custom-call(bf16[128,512]{1,0:T(8,128)(2,1)} %q_nope.1, bf16[128,256]{1,0:T(8,128)(2,1)} %q_rope.1, bf16[128,512]{1,0:T(8,128)(2,1)} %kv.1, bf16[64,128]{1,0:T(8,128)(2,1)} %bitcast.8, bf16[512,512]{1,0:T(8,128)(2,1)} %key_up.1, bf16[512,512]{1,0:T(8,128)(2,1)} %value_up.1, ...), custom_call_target="tpu_custom_call" | custom-call | tf_op jit(solution)/shard_map/layer/pallas_call | solution.py:982
  205.6 1.6 copy.19
  207.2 1.1 copy.20
